TPU v7x, 32 devices: a whole 2x2x4 slice. The times are simulated.
32 devices in a mesh: fsdp: 4 (over y, x), ctx: 2 (over core), tp: 4 (over z).
Axes of the slice: x: 2, y: 2, z: 4, core: 2. Of those that a mesh axis runs over, the one named last changes fastest.
Arguments:
- tokens: bfloat16 [12288, 1024], P(('fsdp', 'ctx', 'tp')), may hold values from -6 to 6
- out_grad: bfloat16 [12288, 1024], P(('fsdp', 'ctx', 'tp')), may hold values from -6 to 6
- block_slot: int32 [4, 6], P('fsdp'), may hold values from 0 to 5, each once within a row
- attn_gain: float32 [1024], replicated, may hold values from 0.5 to 1.5
- ffn_gain: float32 [1024], replicated, may hold values from 0.5 to 1.5
- query_gain: float32 [128], replicated, may hold values from 1 to 2
- key_norm_gain: float32 [128], replicated, may hold values from 1 to 2
- w_query: bfloat16 [1024, 2048], P(('fsdp', 'ctx'), 'tp'), may hold values from -0.1875 to 0.1875
- key_weight: bfloat16 [1024, 1024], P(('fsdp', 'ctx'), 'tp'), may hold values from -0.1875 to 0.1875
- value_weight: bfloat16 [1024, 1024], P(('fsdp', 'ctx'), 'tp'), may hold values from -0.1875 to 0.1875
- w_out: bfloat16 [2048, 1024], P('tp', ('fsdp', 'ctx')), may hold values from -0.5 to 0.5
- w_gate: bfloat16 [1024, 3072], P(('fsdp', 'ctx'), 'tp'), may hold values from -0.1875 to 0.1875
- w_up: bfloat16 [1024, 3072], P(('fsdp', 'ctx'), 'tp'), may hold values from -0.1875 to 0.1875
- w_down: bfloat16 [3072, 1024], P('tp', ('fsdp', 'ctx')), may hold values from -0.21875 to 0.21875
Outputs:
- out: bfloat16 [12288, 1024], P(('fsdp', 'ctx', 'tp'))
- input_grad: float32 [12288, 1024], P(('fsdp', 'ctx', 'tp'))
- attn_gain_grad: float32 [1024], replicated
- ffn_gain_grad: float32 [1024], replicated
- query_gain_grad: float32 [128], replicated
- key_gain_grad: float32 [128], replicated
- w_query_grad: float32 [1024, 2048], P(('fsdp', 'ctx'), 'tp')
- w_key_grad: float32 [1024, 1024], P(('fsdp', 'ctx'), 'tp')
- w_value_grad: float32 [1024, 1024], P(('fsdp', 'ctx'), 'tp')
- w_out_grad: float32 [2048, 1024], P('tp', ('fsdp', 'ctx'))
- w_gate_grad: float32 [1024, 3072], P(('fsdp', 'ctx'), 'tp')
- w_up_grad: float32 [1024, 3072], P(('fsdp', 'ctx'), 'tp')
- w_down_grad: float32 [3072, 1024], P('tp', ('fsdp', 'ctx'))
Inputs may be any that keep to these rules, and one draw needn't show every extreme that they name: `block_slot`: each row names every block of its group once; blocks under 4 are the prompt's in order, the others are continuations.
All inputs are finite; a program needn't handle non-finite values.
Results may differ from a plain program's by a relative error of at most 0.024.
Values may be sent and summed in bfloat16 or wider, within the bound.
A program may use at most 128 MiB of HBM per device.

v0:
```python
import jax
import jax.numpy as jnp
from jax import lax
from jax.sharding import PartitionSpec as P

HEAD_WIDTH = 128
BLOCK_TOKENS = 512
PROMPT = 2048
PBLOCKS = 4


eps_norm = 1e-06
rope_base = 1000000.0


def normed_rows(value):
    return value * lax.rsqrt(jnp.mean(value * value, axis=-1, keepdims=True) + eps_norm)


def norm_back(value, gain, grad):
    inverse = lax.rsqrt(jnp.mean(value * value, axis=-1, keepdims=True) + eps_norm)
    normed = value * inverse
    scaled = grad * gain
    back = inverse * (scaled - normed * jnp.mean(scaled * normed, axis=-1, keepdims=True))
    return (back, grad * normed)


def rotate_half(value, cosine_table, sine_table):
    half = value.shape[-1] // 2
    turned = jnp.concatenate([-value[..., half:], value[..., :half]], axis=-1)
    return value * cosine_table + turned * sine_table


def rotate_back(grad, cosine_table, sine_table):
    half = grad.shape[-1] // 2
    moved = grad * sine_table
    turned = jnp.concatenate([moved[..., half:], -moved[..., :half]], axis=-1)
    return grad * cosine_table + turned


def rope_tables(places):
    freqs = rope_base ** (-(jnp.arange(0, HEAD_WIDTH, 2).astype(jnp.float32) / HEAD_WIDTH))
    angles = places.astype(jnp.float32)[:, None] * freqs[None, :]
    angles = jnp.concatenate([angles, angles], axis=-1)
    return (jnp.cos(angles)[:, None, :], jnp.sin(angles)[:, None, :])


def block_places(block_ids):
    offsets = jnp.arange(BLOCK_TOKENS, dtype=jnp.int32)
    in_prompt = block_ids < PBLOCKS
    start = jnp.where(in_prompt, block_ids * BLOCK_TOKENS, PROMPT)
    places = (start[:, None] + offsets[None, :]).reshape(-1)
    order = jnp.where(in_prompt, 0, block_ids - PBLOCKS + 1)
    groups = jnp.broadcast_to(order[:, None], (block_ids.shape[0], BLOCK_TOKENS)).reshape(-1)
    return (places, groups)


def visible_pair(query_id, key_id):
    return (key_id < PBLOCKS) & ((query_id >= PBLOCKS) | (key_id <= query_id)) | (
        key_id == query_id
    )


def unchanged(state):
    return state


def contract_rows(left, right):
    return lax.dot_general(
        left, right, (((0,), (0,)), ((), ())), preferred_element_type=jnp.float32
    )


def contract_cols(left, right):
    return lax.dot_general(
        left, right, (((1,), (1,)), ((), ())), preferred_element_type=jnp.float32
    )


def on_device(
    tokens,
    out_grad,
    block_slot,
    attn_gain,
    ffn_gain,
    query_gain,
    key_norm_gain,
    w_query,
    key_weight,
    value_weight,
    w_out,
    w_gate,
    w_up,
    w_down,
):
    scale = HEAD_WIDTH ** (-0.5)
    query_full, key_full, value_full, out_full, gate_full, up_full, down_full = (
        lax.all_gather(w_query, ("fsdp", "ctx"), axis=0, tiled=True),
        lax.all_gather(key_weight, ("fsdp", "ctx"), axis=0, tiled=True),
        lax.all_gather(value_weight, ("fsdp", "ctx"), axis=0, tiled=True),
        lax.all_gather(w_out, ("fsdp", "ctx"), axis=1, tiled=True),
        lax.all_gather(w_gate, ("fsdp", "ctx"), axis=0, tiled=True),
        lax.all_gather(w_up, ("fsdp", "ctx"), axis=0, tiled=True),
        lax.all_gather(w_down, ("fsdp", "ctx"), axis=1, tiled=True),
    )
    q_heads = query_full.shape[1] // HEAD_WIDTH
    kv_heads = key_full.shape[1] // HEAD_WIDTH
    repeat = q_heads // kv_heads
    holder = lax.axis_index("ctx")
    block_ids = block_slot[0]
    per_holder = block_ids.shape[0] // lax.axis_size("ctx")
    rows = per_holder * BLOCK_TOKENS
    span = block_ids.shape[0] * BLOCK_TOKENS
    key_places, key_groups = block_places(block_ids)
    query_places = lax.dynamic_slice_in_dim(key_places, holder * rows, rows)
    query_groups = lax.dynamic_slice_in_dim(key_groups, holder * rows, rows)
    inputs = tokens.astype(jnp.float32)
    attn_low = (normed_rows(inputs) * attn_gain).astype(jnp.bfloat16)
    attn_all = lax.all_gather(attn_low, "tp", axis=0, tiled=True)
    query_pre = jnp.dot(attn_all, query_full, preferred_element_type=jnp.float32).reshape(
        rows, q_heads, HEAD_WIDTH
    )
    key_pre = jnp.dot(attn_all, key_full, preferred_element_type=jnp.float32).reshape(
        rows, kv_heads, HEAD_WIDTH
    )
    value_low = jnp.dot(attn_all, value_full, preferred_element_type=jnp.float32).astype(
        jnp.bfloat16
    )
    cosine_table, sine_table = rope_tables(query_places)
    query_rot = rotate_half(normed_rows(query_pre) * query_gain, cosine_table, sine_table).astype(
        jnp.bfloat16
    )
    key_rot = rotate_half(normed_rows(key_pre) * key_norm_gain, cosine_table, sine_table).astype(
        jnp.bfloat16
    )
    key_all, value_all = (
        lax.all_gather(key_rot.reshape(rows, kv_heads * HEAD_WIDTH), "ctx", axis=0, tiled=True),
        lax.all_gather(value_low, "ctx", axis=0, tiled=True),
    )
    key_all = key_all.reshape(span, kv_heads, HEAD_WIDTH)
    value_all = value_all.reshape(span, kv_heads, HEAD_WIDTH)
    query_grp = query_rot.reshape(rows, kv_heads, repeat, HEAD_WIDTH)

    def block_scores(query_blk, q_pos, q_seq, index):
        key_blk = lax.dynamic_slice_in_dim(key_all, index * BLOCK_TOKENS, BLOCK_TOKENS)
        k_pos = lax.dynamic_slice_in_dim(key_places, index * BLOCK_TOKENS, BLOCK_TOKENS)
        k_seq = lax.dynamic_slice_in_dim(key_groups, index * BLOCK_TOKENS, BLOCK_TOKENS)
        scores = (
            jnp.einsum("qkrd,tkd->krqt", query_blk, key_blk, preferred_element_type=jnp.float32)
            * scale
        )
        allowed = (k_pos[None, :] <= q_pos[:, None]) & (
            (k_seq[None, :] == q_seq[:, None]) | (k_seq[None, :] == 0)
        )
        return (scores, allowed)

    def forward_block(local):
        query_blk = lax.dynamic_slice_in_dim(query_grp, local * BLOCK_TOKENS, BLOCK_TOKENS)
        q_pos = lax.dynamic_slice_in_dim(query_places, local * BLOCK_TOKENS, BLOCK_TOKENS)
        q_seq = lax.dynamic_slice_in_dim(query_groups, local * BLOCK_TOKENS, BLOCK_TOKENS)
        query_id = block_ids[holder * per_holder + local]

        def stats_step(index, carry):

            def stats_visit(state):
                peak_old, total = state
                scores, allowed = block_scores(query_blk, q_pos, q_seq, index)
                peak = jnp.maximum(peak_old, jnp.max(jnp.where(allowed, scores, -1e30), axis=-1))
                weights = jnp.exp(jnp.where(allowed, scores - peak[..., None], -1e30))
                return (peak, total * jnp.exp(peak_old - peak) + jnp.sum(weights, axis=-1))

            return lax.cond(visible_pair(query_id, block_ids[index]), stats_visit, unchanged, carry)

        start = (
            jnp.full((kv_heads, repeat, BLOCK_TOKENS), -1e30, jnp.float32),
            jnp.zeros((kv_heads, repeat, BLOCK_TOKENS), jnp.float32),
        )
        peak, total = lax.fori_loop(0, block_ids.shape[0], stats_step, start)
        log_total = peak + jnp.log(total)

        def out_step(index, acc):

            def out_visit(state):
                scores, allowed = block_scores(query_blk, q_pos, q_seq, index)
                probs = jnp.exp(jnp.where(allowed, scores - log_total[..., None], -1e30)).astype(
                    jnp.bfloat16
                )
                value_blk = lax.dynamic_slice_in_dim(value_all, index * BLOCK_TOKENS, BLOCK_TOKENS)
                return state + jnp.einsum(
                    "krqt,tkd->qkrd", probs, value_blk, preferred_element_type=jnp.float32
                )

            return lax.cond(visible_pair(query_id, block_ids[index]), out_visit, unchanged, acc)

        mixed_blk = lax.fori_loop(
            0,
            block_ids.shape[0],
            out_step,
            jnp.zeros((BLOCK_TOKENS, kv_heads, repeat, HEAD_WIDTH), jnp.float32),
        )
        return (mixed_blk, log_total)

    mixed_blocks, log_totals = lax.map(forward_block, jnp.arange(per_holder, dtype=jnp.int32))
    mixed = mixed_blocks.reshape(rows, q_heads * HEAD_WIDTH)
    mixed_low = mixed.astype(jnp.bfloat16)
    state = inputs + lax.psum_scatter(
        jnp.dot(mixed_low, out_full, preferred_element_type=jnp.float32).astype(jnp.bfloat16),
        "tp",
        scatter_dimension=0,
        tiled=True,
    ).astype(jnp.float32)
    ffn_low = (normed_rows(state) * ffn_gain).astype(jnp.bfloat16)
    ffn_all = lax.all_gather(ffn_low, "tp", axis=0, tiled=True)
    gate = jnp.dot(ffn_all, gate_full, preferred_element_type=jnp.float32)
    up_val = jnp.dot(ffn_all, up_full, preferred_element_type=jnp.float32)
    hidden = (jax.nn.silu(gate) * up_val).astype(jnp.bfloat16)
    result = (
        state
        + lax.psum_scatter(
            jnp.dot(hidden, down_full, preferred_element_type=jnp.float32).astype(jnp.bfloat16),
            "tp",
            scatter_dimension=0,
            tiled=True,
        ).astype(jnp.float32)
    ).astype(jnp.bfloat16)
    query_full, key_full, value_full, out_full, gate_full, up_full, down_full = (
        lax.all_gather(w_query, ("fsdp", "ctx"), axis=0, tiled=True),
        lax.all_gather(key_weight, ("fsdp", "ctx"), axis=0, tiled=True),
        lax.all_gather(value_weight, ("fsdp", "ctx"), axis=0, tiled=True),
        lax.all_gather(w_out, ("fsdp", "ctx"), axis=1, tiled=True),
        lax.all_gather(w_gate, ("fsdp", "ctx"), axis=0, tiled=True),
        lax.all_gather(w_up, ("fsdp", "ctx"), axis=0, tiled=True),
        lax.all_gather(w_down, ("fsdp", "ctx"), axis=1, tiled=True),
    )
    grad_all = lax.all_gather(out_grad, "tp", axis=0, tiled=True)
    down_grad = contract_rows(hidden, grad_all)
    hidden_grad = contract_cols(grad_all, down_full)
    sigma = jax.nn.sigmoid(gate)
    up_low = (hidden_grad * gate * sigma).astype(jnp.bfloat16)
    gate_low = (hidden_grad * up_val * sigma * (1.0 + gate * (1.0 - sigma))).astype(jnp.bfloat16)
    gate_grad = contract_rows(ffn_all, gate_low)
    up_grad = contract_rows(ffn_all, up_low)
    ffn_in_grad = lax.psum_scatter(
        (contract_cols(gate_low, gate_full) + contract_cols(up_low, up_full)).astype(jnp.bfloat16),
        "tp",
        scatter_dimension=0,
        tiled=True,
    ).astype(jnp.float32)
    state_back, ffn_gain_part = norm_back(state, ffn_gain, ffn_in_grad)
    state_grad = out_grad.astype(jnp.float32) + state_back
    state_all = lax.all_gather(state_grad.astype(jnp.bfloat16), "tp", axis=0, tiled=True)
    out_weight_grad = contract_rows(mixed_low, state_all)
    mixed_grad = contract_cols(state_all, out_full).astype(jnp.bfloat16)
    mixed_grad_grp = mixed_grad.reshape(rows, kv_heads, repeat, HEAD_WIDTH)
    deltas = jnp.sum(
        mixed_grad_grp.astype(jnp.float32) * mixed.reshape(rows, kv_heads, repeat, HEAD_WIDTH),
        axis=-1,
    )

    def backward_block(local, carry):
        query_acc_all, key_acc, value_acc = carry
        query_blk = lax.dynamic_slice_in_dim(query_grp, local * BLOCK_TOKENS, BLOCK_TOKENS)
        grad_blk = lax.dynamic_slice_in_dim(mixed_grad_grp, local * BLOCK_TOKENS, BLOCK_TOKENS)
        q_pos = lax.dynamic_slice_in_dim(query_places, local * BLOCK_TOKENS, BLOCK_TOKENS)
        q_seq = lax.dynamic_slice_in_dim(query_groups, local * BLOCK_TOKENS, BLOCK_TOKENS)
        delta_blk = jnp.transpose(
            lax.dynamic_slice_in_dim(deltas, local * BLOCK_TOKENS, BLOCK_TOKENS), (1, 2, 0)
        )
        log_total = log_totals[local]
        query_id = block_ids[holder * per_holder + local]

        def key_step(index, state_in):

            def key_visit(state):
                query_acc, key_sum, value_sum = state
                scores, allowed = block_scores(query_blk, q_pos, q_seq, index)
                probs = jnp.exp(jnp.where(allowed, scores - log_total[..., None], -1e30))
                key_blk = lax.dynamic_slice_in_dim(key_all, index * BLOCK_TOKENS, BLOCK_TOKENS)
                value_blk = lax.dynamic_slice_in_dim(value_all, index * BLOCK_TOKENS, BLOCK_TOKENS)
                prob_grad = jnp.einsum(
                    "qkrd,tkd->krqt", grad_blk, value_blk, preferred_element_type=jnp.float32
                )
                score_low = (probs * (prob_grad - delta_blk[..., None])).astype(jnp.bfloat16)
                query_acc = query_acc + scale * jnp.einsum(
                    "krqt,tkd->qkrd", score_low, key_blk, preferred_element_type=jnp.float32
                )
                key_part = scale * jnp.einsum(
                    "krqt,qkrd->tkd", score_low, query_blk, preferred_element_type=jnp.float32
                )
                value_part = jnp.einsum(
                    "krqt,qkrd->tkd",
                    probs.astype(jnp.bfloat16),
                    grad_blk,
                    preferred_element_type=jnp.float32,
                )
                key_sum = lax.dynamic_update_slice_in_dim(
                    key_sum,
                    lax.dynamic_slice_in_dim(key_sum, index * BLOCK_TOKENS, BLOCK_TOKENS)
                    + key_part,
                    index * BLOCK_TOKENS,
                    0,
                )
                value_sum = lax.dynamic_update_slice_in_dim(
                    value_sum,
                    lax.dynamic_slice_in_dim(value_sum, index * BLOCK_TOKENS, BLOCK_TOKENS)
                    + value_part,
                    index * BLOCK_TOKENS,
                    0,
                )
                return (query_acc, key_sum, value_sum)

            return lax.cond(
                visible_pair(query_id, block_ids[index]), key_visit, unchanged, state_in
            )

        start = (
            jnp.zeros((BLOCK_TOKENS, kv_heads, repeat, HEAD_WIDTH), jnp.float32),
            key_acc,
            value_acc,
        )
        query_acc, key_acc, value_acc = lax.fori_loop(0, block_ids.shape[0], key_step, start)
        query_acc_all = lax.dynamic_update_slice_in_dim(
            query_acc_all, query_acc, local * BLOCK_TOKENS, 0
        )
        return (query_acc_all, key_acc, value_acc)

    empty_keys = jnp.zeros((span, kv_heads, HEAD_WIDTH), jnp.float32)
    query_grad, key_sum, value_sum = lax.fori_loop(
        0,
        per_holder,
        backward_block,
        (jnp.zeros((rows, kv_heads, repeat, HEAD_WIDTH), jnp.float32), empty_keys, empty_keys),
    )
    key_own, value_own = (
        lax.psum_scatter(
            key_sum.reshape(span, kv_heads * HEAD_WIDTH).astype(jnp.bfloat16),
            "ctx",
            scatter_dimension=0,
            tiled=True,
        ).astype(jnp.float32),
        lax.psum_scatter(
            value_sum.reshape(span, kv_heads * HEAD_WIDTH).astype(jnp.bfloat16),
            "ctx",
            scatter_dimension=0,
            tiled=True,
        ).astype(jnp.float32),
    )
    query_back, query_gain_part = norm_back(
        query_pre,
        query_gain,
        rotate_back(query_grad.reshape(rows, q_heads, HEAD_WIDTH), cosine_table, sine_table),
    )
    key_back, key_gain_part = norm_back(
        key_pre,
        key_norm_gain,
        rotate_back(key_own.reshape(rows, kv_heads, HEAD_WIDTH), cosine_table, sine_table),
    )
    query_low = query_back.reshape(rows, q_heads * HEAD_WIDTH).astype(jnp.bfloat16)
    key_low = key_back.reshape(rows, kv_heads * HEAD_WIDTH).astype(jnp.bfloat16)
    value_grad_low = value_own.astype(jnp.bfloat16)
    query_weight_grad = contract_rows(attn_all, query_low)
    key_weight_grad = contract_rows(attn_all, key_low)
    value_weight_grad = contract_rows(attn_all, value_grad_low)
    key_part = key_low
    value_part = value_grad_low
    attn_in_grad = lax.psum_scatter(
        (
            contract_cols(query_low, query_full)
            + contract_cols(key_part, key_full)
            + contract_cols(value_part, value_full)
        ).astype(jnp.bfloat16),
        "tp",
        scatter_dimension=0,
        tiled=True,
    ).astype(jnp.float32)
    input_back, attn_gain_part = norm_back(inputs, attn_gain, attn_in_grad)
    input_grad = state_grad + input_back
    grads = (
        lax.psum_scatter(query_weight_grad, ("fsdp", "ctx"), scatter_dimension=0, tiled=True),
        lax.psum_scatter(key_weight_grad, ("fsdp", "ctx"), scatter_dimension=0, tiled=True),
        lax.psum_scatter(value_weight_grad, ("fsdp", "ctx"), scatter_dimension=0, tiled=True),
        lax.psum_scatter(out_weight_grad, ("fsdp", "ctx"), scatter_dimension=1, tiled=True),
        lax.psum_scatter(gate_grad, ("fsdp", "ctx"), scatter_dimension=0, tiled=True),
        lax.psum_scatter(up_grad, ("fsdp", "ctx"), scatter_dimension=0, tiled=True),
        lax.psum_scatter(down_grad, ("fsdp", "ctx"), scatter_dimension=1, tiled=True),
    )
    gains = lax.psum(
        (
            jnp.sum(attn_gain_part, axis=0),
            jnp.sum(ffn_gain_part, axis=0),
            jnp.sum(query_gain_part, axis=(0, 1)),
            jnp.sum(key_gain_part, axis=(0, 1)),
        ),
        ("fsdp", "ctx", "tp"),
    )
    return (
        result,
        input_grad,
        gains[0],
        gains[1],
        gains[2],
        gains[3],
        grads[0],
        grads[1],
        grads[2],
        grads[3],
        grads[4],
        grads[5],
        grads[6],
    )


def solution(mesh):
    placed = (
        P(("fsdp", "ctx", "tp"), None),
        P(("fsdp", "ctx", "tp"), None),
        P("fsdp", None),
        P(),
        P(),
        P(),
        P(),
        P(("fsdp", "ctx"), "tp"),
        P(("fsdp", "ctx"), "tp"),
        P(("fsdp", "ctx"), "tp"),
        P("tp", ("fsdp", "ctx")),
        P(("fsdp", "ctx"), "tp"),
        P(("fsdp", "ctx"), "tp"),
        P("tp", ("fsdp", "ctx")),
    )
    return jax.shard_map(
        on_device,
        mesh=mesh,
        in_specs=placed,
        out_specs=(
            P(("fsdp", "ctx", "tp"), None),
            P(("fsdp", "ctx", "tp"), None),
            P(),
            P(),
            P(),
            P(),
            P(("fsdp", "ctx"), "tp"),
            P(("fsdp", "ctx"), "tp"),
            P(("fsdp", "ctx"), "tp"),
            P("tp", ("fsdp", "ctx")),
            P(("fsdp", "ctx"), "tp"),
            P(("fsdp", "ctx"), "tp"),
            P("tp", ("fsdp", "ctx")),
        ),
        check_vma=False,
    )
```

profile of v0, /device:TPU:0, one launch (start us, length us, event | category | flops | bytes accessed | tf_op | source)
XLA Modules:
  0.0 1494.4 jit_solution(12106573805937478653)
XLA Ops:
  27.2 50.1 %all-gather.12.cloned.1.call-done = bf16[1536,1024]{1,0:T(8,128)(2,1)} async-done(((bf16[384,1024]{1,0:T(8,128)(2,1)}), bf16[1536,1024]{1,0:T(8,128)(2,1)}) %all-gather.12.cloned.1.call-update) | async-done | bytes 3145744 | tf_op jit(solution)/shard_map/all_gather | solution.py:119
  128.9 211.8 %while.124 = (s32[]{:T(128)}, f32[3,512,2,2,128]{1,4,3,2,0:T(8,128)}, f32[3,2,2,512]{3,2,1,0:T(2,128)S(1)}, s32[3]{0:T(128)S(1)}, s32[]{:T(128)}, /*index=5*/s32...) while((s32[]{:T(128)}, ...), condition=%wide.region_14.15_spmd.clone, body=%wide.region_3.14_spmd.clone.sunk | while | flops 819210240 | bytes 18108788 | solution.py:203
  159.5 29.6 %while.128 = (s32[]{:T(128)}, f32[512,2,2,128]{0,3,2,1:T(8,128)S(1)}, s32[6]{0:T(128)S(1)}, s32[]{:T(128)}, pred[]{:T(512)}, /*index=5*/bf16[3072,2,128]{0,2,1:T...) while((s32[]{:T(128)}, ...), condition=%wide.region_13.13_spmd, body=%wide.region_10.12_spmd.sunk | while | flops 542376448 | bytes 3696984 | solution.py:195
  194.7 33.0 %while.127 = (s32[]{:T(128)}, f32[2,2,512]{2,1,0:T(2,128)S(1)}, f32[2,2,512]{2,1,0:T(2,128)S(1)}, s32[6]{0:T(128)S(1)}, s32[]{:T(128)}, /*index=5*/pred[]{:T(512...) while((s32[]{:T(128)}, f32[2,2,512]{2,1,0:T(2,128)S(1)}, ...), condition=%wide.region_9.9_spmd, body=%wide.region_4.8_spmd.sunk | while | flops 276828672 | bytes 10085740 | solution.py:178
  227.9 39.3 %while.128 = (s32[]{:T(128)}, f32[512,2,2,128]{0,3,2,1:T(8,128)S(1)}, s32[6]{0:T(128)S(1)}, s32[]{:T(128)}, pred[]{:T(512)}, /*index=5*/bf16[3072,2,128]{0,2,1:T...) while((s32[]{:T(128)}, ...), condition=%wide.region_13.13_spmd, body=%wide.region_10.12_spmd.sunk | while | flops 542376448 | bytes 3696984 | solution.py:195
  272.7 30.6 %while.127 = (s32[]{:T(128)}, f32[2,2,512]{2,1,0:T(2,128)S(1)}, f32[2,2,512]{2,1,0:T(2,128)S(1)}, s32[6]{0:T(128)S(1)}, s32[]{:T(128)}, /*index=5*/pred[]{:T(512...) while((s32[]{:T(128)}, f32[2,2,512]{2,1,0:T(2,128)S(1)}, ...), condition=%wide.region_9.9_spmd, body=%wide.region_4.8_spmd.sunk | while | flops 276828672 | bytes 10085740 | solution.py:178
  303.5 36.1 %while.128 = (s32[]{:T(128)}, f32[512,2,2,128]{0,3,2,1:T(8,128)S(1)}, s32[6]{0:T(128)S(1)}, s32[]{:T(128)}, pred[]{:T(512)}, /*index=5*/bf16[3072,2,128]{0,2,1:T...) while((s32[]{:T(128)}, ...), condition=%wide.region_13.13_spmd, body=%wide.region_10.12_spmd.sunk | while | flops 542376448 | bytes 3696984 | solution.py:195
  355.7 60.6 %reduce-scatter.14.cloned.1.call-done = bf16[384,1024]{1,0:T(8,128)(2,1)} async-done(((bf16[1536,1024]{1,0:T(8,128)(2,1)}), bf16[384,1024]{1,0:T(8,128)(2,1)}) %reduce-scatter.14.cloned.1.call-update) | async-done | bytes 786448 | tf_op jit(solution)/shard_map/reduce_scatter | solution.py:206
  443.9 65.7 %all-gather.22.cloned.1.call-done = bf16[1536,1024]{1,0:T(8,128)(2,1)} async-done(((bf16[384,1024]{1,0:T(8,128)(2,1)}), bf16[1536,1024]{1,0:T(8,128)(2,1)}) %all-gather.22.cloned.1.call-update) | async-done | bytes 3145744 | tf_op jit(solution)/shard_map/all_gather | solution.py:213
  563.5 65.1 %all-gather.30.cloned.1.call-done = bf16[1536,1024]{1,0:T(8,128)(2,1)} async-done(((bf16[384,1024]{1,0:T(8,128)(2,1)}), bf16[1536,1024]{1,0:T(8,128)(2,1)}) %all-gather.30.cloned.1.call-update) | async-done | bytes 3145744 | tf_op jit(solution)/shard_map/all_gather | solution.py:235
  646.9 59.0 %reduce-scatter.18.cloned.1.call-done = bf16[384,1024]{1,0:T(8,128)(2,1)} async-done(((bf16[1536,1024]{1,0:T(8,128)(2,1)}), bf16[384,1024]{1,0:T(8,128)(2,1)}) %reduce-scatter.18.cloned.1.call-update) | async-done | bytes 786448 | tf_op jit(solution)/shard_map/reduce_scatter | solution.py:243
  717.2 56.5 %all-gather.32.cloned.1.call-done = bf16[1536,1024]{1,0:T(8,128)(2,1)} async-done(((bf16[384,1024]{1,0:T(8,128)(2,1)}), bf16[1536,1024]{1,0:T(8,128)(2,1)}) %all-gather.32.cloned.1.call-update) | async-done | bytes 3145744 | tf_op jit(solution)/shard_map/all_gather | solution.py:251
  800.7 197.2 %while.126 = (s32[]{:T(128)}, f32[1536,2,2,128]{0,3,2,1:T(8,128)}, f32[3072,2,128]{2,0,1:T(8,128)}, f32[3072,2,128]{2,0,1:T(8,128)}, s32[]{:T(128)}, /*index=5*/...) while((s32[]{:T(128)}, f32[1536,2,2,128]{0,3,2,1:T(8,128)}, ...), condition=%wide.region_26.27_spmd.clone, body=%wide.region_21.26_spmd.clone.sunk | while | flops 1354632704 | bytes 35285052 | solution.py:328
  805.7 42.6 %while.129 = (s32[]{:T(128)}, f32[512,2,2,128]{0,3,2,1:T(8,128)S(1)}, f32[3072,2,128]{2,0,1:T(8,128)}, f32[3072,2,128]{2,0,1:T(8,128)}, s32[6]{0:T(128)S(1)}, /*...) while((s32[]{:T(128)}, ...), condition=%wide.region_25.25_spmd, body=%wide.region_22.24_spmd.sunk | while | flops 1354629632 | bytes 28878328 | solution.py:321
  854.2 73.4 %while.129 = (s32[]{:T(128)}, f32[512,2,2,128]{0,3,2,1:T(8,128)S(1)}, f32[3072,2,128]{2,0,1:T(8,128)}, f32[3072,2,128]{2,0,1:T(8,128)}, s32[6]{0:T(128)S(1)}, /*...) while((s32[]{:T(128)}, ...), condition=%wide.region_25.25_spmd, body=%wide.region_22.24_spmd.sunk | while | flops 1354629632 | bytes 28878328 | solution.py:321
  933.7 63.2 %while.129 = (s32[]{:T(128)}, f32[512,2,2,128]{0,3,2,1:T(8,128)S(1)}, f32[3072,2,128]{2,0,1:T(8,128)}, f32[3072,2,128]{2,0,1:T(8,128)}, s32[6]{0:T(128)S(1)}, /*...) while((s32[]{:T(128)}, ...), condition=%wide.region_25.25_spmd, body=%wide.region_22.24_spmd.sunk | while | flops 1354629632 | bytes 28878328 | solution.py:321
  1103.8 45.0 %all-reduce = (f32[1024]{0:T(1024)}, f32[1024]{0:T(1024)}, f32[128]{0:T(128)}, f32[128]{0:T(128)}) all-reduce(f32[1024]{0:T(1024)S(1)} %get-tuple-element.1859, f32[1024]{0:T(1024)S(1)} %copy-done.43, f32[128]{0:T(128)S(1)} %get-tuple-element.1855, ...), channel_id=1, replica_groups=mesh['fsdp'=4,'ctx'=2,'tp'=4] {'fsdp','ctx','tp'}, use_global_device_ids=true, to_apply=%region_34.35 | all-reduce | flops 2304 | bytes 18432 | tf_op jit(solution)/shard_map/psum | solution.py:387
  1169.5 46.1 %reduce-scatter.38.cloned.1.call-done = f32[768,128]{1,0:T(8,128)} async-done(((f32[768,1024]{1,0:T(8,128)}), f32[768,128]{1,0:T(8,128)}) %reduce-scatter.38.cloned.1.call-update) | async-done | bytes 393232 | tf_op jit(solution)/shard_map/reduce_scatter | solution.py:385
  1215.6 50.6 %reduce-scatter.34.cloned.1.call-done = f32[128,768]{1,0:T(8,128)} async-done(((f32[1024,768]{1,0:T(8,128)}), f32[128,768]{1,0:T(8,128)}) %reduce-scatter.34.cloned.1.call-update) | async-done | bytes 393232 | tf_op jit(solution)/shard_map/reduce_scatter | solution.py:383
  1266.3 50.1 %reduce-scatter.36.cloned.1.call-done = f32[128,768]{1,0:T(8,128)} async-done(((f32[1024,768]{1,0:T(8,128)}), f32[128,768]{1,0:T(8,128)}) %reduce-scatter.36.cloned.1.call-update) | async-done | bytes 393232 | tf_op jit(solution)/shard_map/reduce_scatter | solution.py:384
  1316.3 45.5 %reduce-scatter.32.cloned.1.call-done = f32[512,128]{1,0:T(8,128)} async-done(((f32[512,1024]{1,0:T(8,128)}), f32[512,128]{1,0:T(8,128)}) %reduce-scatter.32.cloned.1.call-update) | async-done | bytes 262160 | tf_op jit(solution)/shard_map/reduce_scatter | solution.py:382
  1361.8 45.1 %reduce-scatter.26.cloned.1.call-done = f32[128,512]{1,0:T(8,128)} async-done(((f32[1024,512]{1,0:T(8,128)}), f32[128,512]{1,0:T(8,128)}) %reduce-scatter.26.cloned.1.call-update) | async-done | bytes 262160 | tf_op jit(solution)/shard_map/reduce_scatter | solution.py:379
  1406.9 40.1 %reduce-scatter.30.cloned.1.call-done = f32[128,256]{1,0:T(8,128)} async-done(((f32[1024,256]{1,0:T(8,128)}), f32[128,256]{1,0:T(8,128)}) %reduce-scatter.30.cloned.1.call-update) | async-done | bytes 131088 | tf_op jit(solution)/shard_map/reduce_scatter | solution.py:381
  1447.0 40.0 %reduce-scatter.28.cloned.1.call-done = f32[128,256]{1,0:T(8,128)} async-done(((f32[1024,256]{1,0:T(8,128)}), f32[128,256]{1,0:T(8,128)}) %reduce-scatter.28.cloned.1.call-update) | async-done | bytes 131088 | tf_op jit(solution)/shard_map/reduce_scatter | solution.py:380
  (698 shorter events, 783.5 us)
Async XLA Ops:
  7.2 70.1 %all-gather.12.cloned.1.call-start = ((), (), s32[]{:S(2)}) async-start(), calls=%async_computation.13 | async-start | bytes 3932160 | tf_op jit(solution)/shard_map/all_gather | solution.py:119
  10.9 91.0 %all-gather.14.cloned.1.call-start = ((), (), s32[]{:S(2)}) async-start(), calls=%async_computation.14 | async-start | bytes 1179648 | tf_op jit(solution)/shard_map/all_gather | solution.py:98
  11.7 103.4 %all-gather.16.cloned.1.call-start = ((), (), s32[]{:S(2)}) async-start(), calls=%async_computation.15 | async-start | bytes 2359296 | tf_op jit(solution)/shard_map/all_gather | solution.py:137
  82.8 43.5 %all-gather.18.cloned.1.call-start = ((), (), s32[]{:S(2)}) async-start(), calls=%async_computation.16 | async-start | bytes 2359296 | tf_op jit(solution)/shard_map/all_gather | solution.py:138
  97.2 252.3 %all-gather.20.cloned.1.call-start = ((), (), s32[]{:S(2)}) async-start(), calls=%async_computation.17 | async-start | bytes 1179648 | tf_op jit(solution)/shard_map/all_gather | solution.py:101
  97.8 318.5 %reduce-scatter.14.cloned.1.call-start = ((), (), s32[]{:S(2)}) async-start(), calls=%async_computation.18 | async-start | bytes 3932160 | tf_op jit(solution)/shard_map/reduce_scatter | solution.py:206
  354.7 89.2 %all-gather.26.cloned.1.call-start = ((), (), s32[]{:S(2)}) async-start(), calls=%async_computation.21 | async-start | bytes 1769472 | tf_op jit(solution)/shard_map/all_gather | solution.py:103
  355.4 154.2 %all-gather.22.cloned.1.call-start = ((), (), s32[]{:S(2)}) async-start(), calls=%async_computation.19 | async-start | bytes 3932160 | tf_op jit(solution)/shard_map/all_gather | solution.py:213
  420.1 115.8 %all-gather.24.cloned.1.call-start = ((), (), s32[]{:S(2)}) async-start(), calls=%async_computation.20 | async-start | bytes 1769472 | tf_op jit(solution)/shard_map/all_gather | solution.py:102
  420.8 142.7 %all-gather.28.cloned.1.call-start = ((), (), s32[]{:S(2)}) async-start(), calls=%async_computation.22 | async-start | bytes 1769472 | tf_op jit(solution)/shard_map/all_gather | solution.py:104
  421.4 207.2 %all-gather.30.cloned.1.call-start = ((), (), s32[]{:S(2)}) async-start(), calls=%async_computation.24 | async-start | bytes 3932160 | tf_op jit(solution)/shard_map/all_gather | solution.py:235
  422.1 283.7 %reduce-scatter.18.cloned.1.call-start = ((), (), s32[]{:S(2)}) async-start(), calls=%async_computation.25 | async-start | bytes 3932160 | tf_op jit(solution)/shard_map/reduce_scatter | solution.py:243
  646.8 126.9 %all-gather.32.cloned.1.call-start = ((), (), s32[]{:S(2)}) async-start(), calls=%async_computation.26 | async-start | bytes 3932160 | tf_op jit(solution)/shard_map/all_gather | solution.py:251
  710.0 317.4 %reduce-scatter.20.cloned.1.call-start = ((), (), s32[]{:S(2)}) async-start(), calls=%async_computation.27 | async-start | bytes 2359296 | tf_op jit(solution)/shard_map/reduce_scatter | solution.py:335
  1001.6 34.3 %reduce-scatter.22.cloned.1.call-start = ((), (), s32[]{:S(2)}) async-start(), calls=%async_computation.28 | async-start | bytes 2359296 | tf_op jit(solution)/shard_map/reduce_scatter | solution.py:341
  1009.4 92.6 %reduce-scatter.24.cloned.1.call-start = ((), (), s32[]{:S(2)}) async-start(), calls=%async_computation.29 | async-start | bytes 3932160 | tf_op jit(solution)/shard_map/reduce_scatter | solution.py:366
  1043.5 122.0 %reduce-scatter.16.cloned.1.call-start = ((), (), s32[]{:S(2)}) async-start(), calls=%async_computation.23 | async-start | bytes 3932160 | tf_op jit(solution)/shard_map/reduce_scatter | solution.py:219
  1050.6 165.0 %reduce-scatter.38.cloned.1.call-start = ((), (), s32[]{:S(2)}) async-start(), calls=%async_computation.36 | async-start | bytes 3538944 | tf_op jit(solution)/shard_map/reduce_scatter | solution.py:385
  1057.9 208.4 %reduce-scatter.34.cloned.1.call-start = ((), (), s32[]{:S(2)}) async-start(), calls=%async_computation.34 | async-start | bytes 3538944 | tf_op jit(solution)/shard_map/reduce_scatter | solution.py:383
  1065.0 251.3 %reduce-scatter.36.cloned.1.call-start = ((), (), s32[]{:S(2)}) async-start(), calls=%async_computation.35 | async-start | bytes 3538944 | tf_op jit(solution)/shard_map/reduce_scatter | solution.py:384
  1072.0 289.8 %reduce-scatter.32.cloned.1.call-start = ((), (), s32[]{:S(2)}) async-start(), calls=%async_computation.33 | async-start | bytes 2359296 | tf_op jit(solution)/shard_map/reduce_scatter | solution.py:382
  1077.7 329.2 %reduce-scatter.26.cloned.1.call-start = ((), (), s32[]{:S(2)}) async-start(), calls=%async_computation.30 | async-start | bytes 2359296 | tf_op jit(solution)/shard_map/reduce_scatter | solution.py:379
  1083.0 364.0 %reduce-scatter.30.cloned.1.call-start = ((), (), s32[]{:S(2)}) async-start(), calls=%async_computation.32 | async-start | bytes 1179648 | tf_op jit(solution)/shard_map/reduce_scatter | solution.py:381
  1087.0 400.0 %reduce-scatter.28.cloned.1.call-start = ((), (), s32[]{:S(2)}) async-start(), calls=%async_computation.31 | async-start | bytes 1179648 | tf_op jit(solution)/shard_map/reduce_scatter | solution.py:380
  (67 other events, 1351.1 us)
Sparse Core Ops, SparseCore 0:
  11.0 66.1 all-gather.11
  79.2 22.6 all-gather.13
  104.0 9.8 all-gather.15
  115.3 10.9 all-gather.17
  128.1 24.7 all-gather.19
  354.8 61.4 reduce-scatter.13
  418.1 25.7 all-gather.25
  446.0 63.4 all-gather.21
  511.5 24.3 all-gather.23
  537.6 25.8 all-gather.27
  565.1 63.4 all-gather.29
  646.9 58.8 reduce-scatter.17
  710.1 63.5 all-gather.31
  1001.7 7.7 reduce-scatter.19
  1011.8 10.2 reduce-scatter.21
  1043.6 58.3 reduce-scatter.23
  1104.2 61.2 reduce-scatter.15
  1169.4 46.2 reduce-scatter.37
  1220.0 46.2 reduce-scatter.33
  1270.1 46.2 reduce-scatter.35
  1320.5 41.1 reduce-scatter.31
  1365.6 41.2 reduce-scatter.25
  1411.0 36.0 reduce-scatter.29
  1451.0 36.0 reduce-scatter.27
where the time goes:
time: 1510 us; the launch traced here: 1490 us
  waiting for transfers between devices  780 us (52%)
  matrix products  260 us (17%)
  loops' own time  177 us (12%)
  local copies, waits for them, and re-layouts  111 us (7%)
  other arithmetic  80.5 us (5%)
  blocking collectives  67.7 us (4%)
  between operations  15.7 us (1%)
    all_gather x1, waiting for transfers between devices, on_device(): ffn_all = lax.all_gather(ffn_low, 'tp', axis=0, tiled=True)  65.7 us
    all_gather x1, waiting for transfers between devices, on_device(): grad_all = lax.all_gather(out_grad, 'tp', axis=0, tiled=True)  65.1 us
    reduce_scatter x1, waiting for transfers between devices, on_device(): lax.psum_scatter(jnp.dot(mixed_low, out_full, preferred_element_type=jnp....  60.6 us
    reduce_scatter x1, waiting for transfers between devices, on_device(): lax.psum_scatter((contract_cols(gate_low, gate_full) + contract_cols(up_l...  59 us
    another operation x3, loops' own time, forward_block(): lax.fori_loop(0, block_ids.shape[0], out_step, jnp.zeros((BLOCK_TOKENS, k...  58.8 us
    all_gather x1, waiting for transfers between devices, on_device(): lax.all_gather(state_grad.astype(jnp.bfloat16), 'tp', axis=0, tiled=True)  56.5 us
    another operation x3, loops' own time, backward_block(): lax.fori_loop(0, block_ids.shape[0], key_step, start)  54.8 us
    another operation x3, loops' own time, forward_block(): peak, total = lax.fori_loop(0, block_ids.shape[0], stats_step, start)  53.4 us
  transfers between devices with their start and end apart: 24, of which 20 were waited for; matrix products, arithmetic and copies ran while one was open for 16% of the time, Pallas kernels for 0%

commit v1 on v0

v1 whole, which is shorter than its diff:
```python
import math
import jax
import jax.numpy as jnp
from jax import lax
from jax.experimental import pallas as pl
from jax.experimental.pallas import tpu as pltpu
from jax.sharding import PartitionSpec as P

HEAD = 128
BLOCK = 512
PBLOCKS = 4
BLOCKS = 6
EPS = 1e-6
ROPE_BASE = 1e6
MESH = pl.DeviceIdType.MESH
F32, BF16 = jnp.float32, jnp.bfloat16
LOG2E = 1.4426950408889634
QSCALE = HEAD ** -0.5 * LOG2E
VMEM_SPEC = pl.BlockSpec(memory_space=pltpu.VMEM)
ANY_SPEC = pl.BlockSpec(memory_space=pl.ANY)
SMEM_SPEC = pl.BlockSpec(memory_space=pltpu.SMEM)
VMEM_LIMIT = 60 * 2**20


def dot(a, b, dims):
    return lax.dot_general(a, b, (dims, ((), ())), preferred_element_type=F32)


NN = ((1,), (0,))
NT = ((1,), (1,))
TN = ((0,), (0,))


def flip(f, mask):
    bit = 1
    while bit <= mask:
        if mask & bit:
            f = f + bit - 2 * bit * lax.rem(lax.div(f, bit), 2)
        bit *= 2
    return f


def remote(src, dst, send, recv, **where):
    return pltpu.make_async_remote_copy(
        src_ref=src, dst_ref=dst, send_sem=send, recv_sem=recv,
        device_id=where, device_id_type=MESH)


def pick(index, values):
    out = jnp.int32(values[-1])
    for k in range(len(values) - 1):
        out = jnp.where(index == k, jnp.int32(values[k]), out)
    return out


def near_order(n):
    return [sorted(range(n), key=lambda s: (abs(s - z), s)) for z in range(n)]


def bit_orders(fs):
    bits = [1 << b for b in range(fs.bit_length() - 1)]
    return bits, bits[::-1]


def combos(bits):
    out = [0]
    for b in bits:
        out = out + [m + b for m in out]
    return out


def plane_copies(half, stage, fs, f, view, ssem, rsem):
    order = bit_orders(fs)[half]
    partner = flip(f, order[stage])
    base = (1 << stage) - 1
    out = []
    for m, mask in enumerate(combos(order[:stage])):
        g = flip(f, mask)
        out.append(remote(view(g), view(g), ssem.at[base + m], rsem.at[base + m], fsdp=partner))
    return out
def head_norm_rope(pre, gain, cos, sins):
    n = pre * lax.rsqrt(jnp.mean(pre * pre, axis=-1, keepdims=True) + EPS) * gain
    return n * cos + pltpu.roll(n, HEAD // 2, 1) * sins


def gather_kernel(dims, x_ref, dy_ref, gain_ref, wqkv_ref, wz_ref, cos_ref, sin_ref, qg_ref, kg_ref,
                  a_ref, q_ref, k_ref, v_ref, pre_ref, wall_ref, w_ref, dyp_ref,
                  zs, zr, cs, cr, ws, wr, ms, mr, ps, pr, ls):
    fs, nc, nz = dims
    f, c, z = lax.axis_index("fsdp"), lax.axis_index("ctx"), lax.axis_index("tp")
    o = 1 - c
    me = f * nc + c
    others = [(df, dc) for df in range(fs) for dc in range(nc) if (df, dc) != (0, 0)]

    barrier = pltpu.get_barrier_semaphore()
    for df, dc in others:
        pl.semaphore_signal(barrier, inc=1, device_id={"fsdp": lax.rem(f + df, fs), "ctx": lax.rem(c + dc, nc)}, device_id_type=MESH)

    @pl.when(z > 0)
    def _():
        pl.semaphore_signal(barrier, inc=1, device_id={"tp": z - 1}, device_id_type=MESH)

    @pl.when(z < nz - 1)
    def _():
        pl.semaphore_signal(barrier, inc=1, device_id={"tp": z + 1}, device_id_type=MESH)
    own_w = pltpu.make_async_copy(wz_ref.at[c], w_ref.at[z, f, c], ls.at[0])
    own_w.start()
    own_dy = pltpu.make_async_copy(dy_ref, dyp_ref.at[c], ls.at[1])
    own_dy.start()
    x = x_ref[...].astype(F32)
    a_ref[c * nz + z] = (x * lax.rsqrt(jnp.mean(x * x, axis=-1, keepdims=True) + EPS) * gain_ref[...]).astype(BF16)
    wall_ref[me] = wqkv_ref[c]
    pl.semaphore_wait(barrier, len(others) + jnp.where(z > 0, 1, 0) + jnp.where(z < nz - 1, 1, 0))

    row = a_ref.at[c * nz + z]
    up = remote(row, row, zs.at[z], zr.at[z], tp=jnp.minimum(z + 1, nz - 1))
    down = remote(row, row, zs.at[nz], zr.at[z], tp=jnp.maximum(z - 1, 0))
    pl.when(z < nz - 1)(up.start)
    pl.when(z > 0)(down.start)
    across = remote(row, row, cs.at[z], cr.at[z], ctx=o)
    across.start()
    for i, (df, dc) in enumerate(others):
        tf, tc = lax.rem(f + df, fs), lax.rem(c + dc, nc)
        remote(wqkv_ref.at[tc], wall_ref.at[me], ws.at[i], wr.at[me], fsdp=tf, ctx=tc).start()
    half = remote(wz_ref.at[o], w_ref.at[z, f, c], ms.at[0], mr.at[0], ctx=o)
    half.start()
    dyc = remote(dy_ref, dyp_ref.at[c], ms.at[1], mr.at[1], ctx=o)
    dyc.start()

    def plane(half_index, stage):
        return plane_copies(half_index, stage, fs, f, lambda g: w_ref.at[z, g, half_index], ps.at[half_index], pr.at[half_index])
    stages = fs.bit_length() - 1

    own_w.wait()
    remote(wz_ref.at[0], w_ref.at[z, f, o], ms.at[0], mr.at[0], ctx=o).wait_recv()
    for hi in range(2):
        for cp in plane(hi, 0):
            cp.start()
    q_cols = q_ref.shape[-1]

    def project(s):
        y = dot(a_ref[s], wall_ref[...].reshape(-1, wall_ref.shape[2]), NN)
        pre_ref[s] = y[:, :q_cols + HEAD].astype(BF16)
        cos, sins = cos_ref[s], sin_ref[s]
        for h in range(q_cols // HEAD):
            q_ref[s, :, h * HEAD:(h + 1) * HEAD] = (head_norm_rope(y[:, h * HEAD:(h + 1) * HEAD], qg_ref[...], cos, sins) * QSCALE).astype(BF16)
        k_ref[s] = head_norm_rope(y[:, q_cols:q_cols + HEAD], kg_ref[...], cos, sins).astype(BF16)
        v_ref[s, :, :HEAD] = y[:, q_cols + HEAD:].astype(BF16)
        v_ref[s, :, HEAD:] = jnp.ones_like(v_ref[s, :, HEAD:])

    def take(hop):
        @pl.loop(0, 2 if hop == 0 else 4)
        def _(i):
            across_, way = (i, 0) if hop == 0 else (lax.rem(i, 2), lax.div(i, 2))
            src = z + (2 * way - 1) * hop

            @pl.when((src >= 0) & (src < nz))
            def _():
                s = jnp.where(across_ == 0, c, o) * nz + src

                @pl.when(across_ == 1)
                def _():
                    remote(a_ref.at[s], a_ref.at[s], cs.at[src], cr.at[src], ctx=o).wait_recv()
                project(s)

    for hop in range(1, nz):
        for way in range(2):
            src = z + (2 * way - 1) * hop

            @pl.when((src >= 0) & (src < nz))
            def _():
                part = a_ref.at[c * nz + src]
                remote(part, part, zs.at[src], zr.at[src], ctx=o).wait_recv()
                if way == 0:
                    pl.when(z < nz - 1)(remote(part, part, zs.at[src], zr.at[src], tp=jnp.minimum(z + 1, nz - 1)).start)
                else:
                    pl.when(z > 0)(remote(part, part, zs.at[src], zr.at[src], tp=jnp.maximum(z - 1, 0)).start)
                remote(part, part, cs.at[src], cr.at[src], ctx=o).start()
        if hop == 1:
            for i, (df, dc) in enumerate(others):
                src = lax.rem(f + df, fs) * nc + lax.rem(c + dc, nc)
                remote(wqkv_ref.at[0], wall_ref.at[src], ws.at[i], wr.at[src], ctx=o).wait_recv()
        take(hop - 1)
        stage = hop - 1
        if stage < stages:
            for hi in range(2):
                for cp in plane(hi, stage):
                    cp.wait_recv()
                if stage + 1 < stages:
                    for cp in plane(hi, stage + 1):
                        cp.start()
    take(nz - 1)
    for stage in range(nz - 1, stages):
        for hi in range(2):
            for cp in plane(hi, stage):
                cp.wait_recv()
            if stage + 1 < stages:
                for cp in plane(hi, stage + 1):
                    cp.start()
    for stage in range(stages):
        for hi in range(2):
            for cp in plane(hi, stage):
                cp.wait_send()
    for src in range(nz):
        @pl.when(((src <= z) & (z < nz - 1)) | ((src > z) & (z > 0)))
        def _():
            remote(row, row, zs.at[src], zr.at[src], ctx=o).wait_send()
        remote(row, row, cs.at[src], cr.at[src], ctx=o).wait_send()

    @pl.when(z > 0)
    def _():
        remote(row, row, zs.at[nz], zr.at[0], ctx=o).wait_send()
    for i in range(len(others)):
        remote(wqkv_ref.at[0], wall_ref.at[0], ws.at[i], wr.at[0], ctx=o).wait_send()
    half.wait_send()
    dyc.wait_send()
    own_dy.wait()
    remote(dy_ref, dyp_ref.at[o], ms.at[1], mr.at[1], ctx=o).wait_recv()


def gather_call(dims, x, dy, gain, wqkv, wz, cos, sin, qg, kg):
    fs, nc, nz = dims
    rows, width = x.shape
    ns = nc * nz
    cols = wqkv.shape[2]
    q_cols = cols - 2 * HEAD
    DMA = pltpu.SemaphoreType.DMA
    return pl.pallas_call(
        lambda *refs: gather_kernel(dims, *refs),
        out_shape=(
            jax.ShapeDtypeStruct((ns, rows, width), BF16),
            jax.ShapeDtypeStruct((ns, rows, q_cols), BF16),
            jax.ShapeDtypeStruct((ns, rows, HEAD), BF16),
            jax.ShapeDtypeStruct((ns, rows, 2 * HEAD), BF16),
            jax.ShapeDtypeStruct((ns, rows, q_cols + HEAD), BF16),
            jax.ShapeDtypeStruct((fs * nc,) + wqkv.shape[1:], BF16),
            jax.ShapeDtypeStruct((nz, fs, nc) + wz.shape[1:], BF16),
            jax.ShapeDtypeStruct((nc, rows, width), BF16),
        ),
        in_specs=[VMEM_SPEC, ANY_SPEC, VMEM_SPEC, VMEM_SPEC, ANY_SPEC] + [VMEM_SPEC] * 4,
        out_specs=(VMEM_SPEC,) * 6 + (ANY_SPEC, ANY_SPEC),
        scratch_shapes=[
            DMA((nz + 1,)), DMA((nz,)), DMA((nz,)), DMA((nz,)),
            DMA((fs * nc - 1,)), DMA((fs * nc,)), DMA((2,)), DMA((2,)),
            DMA((2, fs - 1)), DMA((2, fs - 1)), DMA((2,)),
        ],
        compiler_params=pltpu.CompilerParams(collective_id=0, has_side_effects=True, vmem_limit_bytes=VMEM_LIMIT),
        cost_estimate=pl.CostEstimate(flops=2 * ns * rows * width * cols, bytes_accessed=30 * 2**20, transcendentals=0),
    )(x, dy, gain, wqkv, wz, cos, sin, qg, kg)
def full_keys(qb):
    return min(qb, PBLOCKS)


def stack_heads(rows):
    return jnp.concatenate([rows[:, h * HEAD:(h + 1) * HEAD] for h in range(rows.shape[1] // HEAD)], axis=0)


def attend_kernel(dims, slot_ref, block_ref, q_ref, k_ref, v_ref, wi_ref, w_ref, or_ref, o_ref, l_ref,
                  ob, zs, zr, ps, pr, xs, xr):
    fs, nc, nz = dims
    f, c, z = lax.axis_index("fsdp"), lax.axis_index("ctx"), lax.axis_index("tp")
    rows = or_ref.shape[2]
    barrier = pltpu.get_barrier_semaphore()
    bits = bit_orders(fs)[0]
    for bit in bits:
        pl.semaphore_signal(barrier, inc=1, device_id={"fsdp": flip(f, bit)}, device_id_type=MESH)
    for dz in range(1, nz):
        pl.semaphore_signal(barrier, inc=1, device_id={"tp": lax.rem(z + dz, nz)}, device_id_type=MESH)
    pl.semaphore_wait(barrier, len(bits) + nz - 1)

    def up(src, sem):
        part = w_ref.at[src, f]
        return remote(part, part, zs.at[sem], zr.at[src], tp=jnp.minimum(z + 1, nz - 1))

    def down(src, sem):
        part = w_ref.at[src, f]
        return remote(part, part, zs.at[sem], zr.at[src], tp=jnp.maximum(z - 1, 0))
    pl.when(z < nz - 1)(up(z, z).start)
    pl.when(z > 0)(down(z, nz).start)
    stages = fs.bit_length() - 1

    def plane(src, hi, stage):
        return plane_copies(hi, stage, fs, f, lambda g: w_ref.at[src, g, hi], ps.at[src, hi], pr.at[src, hi])

    def each(hop, act):
        for way in range(2):
            src = z + (2 * way - 1) * hop

            @pl.when((src >= 0) & (src < nz))
            def _():
                act(way, src)

    def arrive(hop):
        def act(way, src):
            up(src, src).wait_recv()
            if way == 0:
                pl.when(z < nz - 1)(up(src, src).start)
            else:
                pl.when(z > 0)(down(src, src).start)
            for hi in range(2):
                for cp in plane(src, hi, 0):
                    cp.start()
        each(hop, act)

    def spread(hop, stage):
        def act(way, src):
            for hi in range(2):
                for cp in plane(src, hi, stage):
                    cp.wait_recv()
                if stage + 1 < stages:
                    for cp in plane(src, hi, stage + 1):
                        cp.start()
        each(hop, act)

    tri = lax.broadcasted_iota(jnp.int32, (BLOCK, BLOCK), 0) >= lax.broadcasted_iota(jnp.int32, (BLOCK, BLOCK), 1)
    heads = q_ref.shape[2] // HEAD
    for qb in range(BLOCKS):
        q2 = stack_heads(q_ref[slot_ref[qb]])

        def step(kb, acc):
            k = k_ref[slot_ref[kb]]
            v = v_ref[slot_ref[kb]]
            return acc + dot(jnp.exp2(dot(q2, k, NT)).astype(BF16), v, NN)
        acc = jnp.zeros((heads * BLOCK, 2 * HEAD), F32)
        if full_keys(qb):
            acc = lax.fori_loop(0, full_keys(qb), step, acc)
        k = k_ref[slot_ref[qb]]
        v = v_ref[slot_ref[qb]]
        s = dot(q2, k, NT)
        for h in range(heads):
            part = slice(h * BLOCK, (h + 1) * BLOCK)
            p = jnp.where(tri, jnp.exp2(s[part]), 0.0).astype(BF16)
            a = acc[part] + dot(p, v, NN)
            ob[qb, :, h * HEAD:(h + 1) * HEAD] = (a[:, :HEAD] / a[:, HEAD:]).astype(BF16)
            l_ref[qb, :, part] = jnp.log2(a[:, HEAD:]).T[0:8]
    for s in range(BLOCKS):
        o_ref[s * BLOCK:(s + 1) * BLOCK] = ob[block_ref[s]]

    def part_rows(side, zz):
        return pl.ds(pl.multiple_of((side * nz + zz) * rows, 128), rows)
    for dz in range(1, nz):
        to = lax.rem(z + dz, nz)
        for side in range(nc):
            remote(o_ref.at[part_rows(side, to)], or_ref.at[z, side], xs.at[dz, side], xr.at[z, side], tp=to).start()
    for side in range(nc):
        or_ref[z, side] = o_ref[part_rows(side, z)]
    arrive(1)
    for hop in range(1, nz):
        for stage in range(stages):
            if stage == 1 and hop + 1 < nz:
                arrive(hop + 1)
            spread(hop, stage)
        if stages < 2 and hop + 1 < nz:
            arrive(hop + 1)
    for dz in range(1, nz):
        src = lax.rem(z + dz, nz)
        for side in range(nc):
            cp = remote(o_ref.at[part_rows(side, 0)], or_ref.at[src, side], xs.at[dz, side], xr.at[src, side], tp=src)
            cp.wait_recv()
            cp.wait_send()
    for hop in range(1, nz):
        def left(way, src):
            if way == 0:
                pl.when(z < nz - 1)(up(src, src).wait_send)
            else:
                pl.when(z > 0)(down(src, src).wait_send)
            for hi in range(2):
                for stage in range(stages):
                    for cp in plane(src, hi, stage):
                        cp.wait_send()
        each(hop, left)
    pl.when(z < nz - 1)(up(z, z).wait_send)
    pl.when(z > 0)(down(z, nz).wait_send)


def attend_call(dims, slot, block, q, k, v, w, rows):
    fs, nc, nz = dims
    q_cols = q.shape[2]
    span = BLOCKS * BLOCK
    heads = q_cols // HEAD
    DMA = pltpu.SemaphoreType.DMA
    return pl.pallas_call(
        lambda *refs: attend_kernel(dims, *refs),
        out_shape=(
            jax.ShapeDtypeStruct(w.shape, BF16),
            jax.ShapeDtypeStruct((nz, nc, rows, q_cols), BF16),
            jax.ShapeDtypeStruct((span, q_cols), BF16),
            jax.ShapeDtypeStruct((BLOCKS, 8, heads * BLOCK), F32),
        ),
        in_specs=[SMEM_SPEC, SMEM_SPEC] + [VMEM_SPEC] * 3 + [ANY_SPEC],
        out_specs=(ANY_SPEC, VMEM_SPEC, VMEM_SPEC, VMEM_SPEC),
        scratch_shapes=[
            pltpu.VMEM((BLOCKS, BLOCK, q_cols), BF16),
            DMA((nz + 1,)), DMA((nz,)), DMA((nz, 2, fs - 1)), DMA((nz, 2, fs - 1)), DMA((nz, nc)), DMA((nz, nc)),
        ],
        input_output_aliases={5: 0},
        compiler_params=pltpu.CompilerParams(collective_id=1, has_side_effects=True, vmem_limit_bytes=VMEM_LIMIT),
        cost_estimate=pl.CostEstimate(flops=2 * 20 * BLOCK * BLOCK * heads * 3 * HEAD, bytes_accessed=30 * 2**20, transcendentals=0),
    )(slot, block, q, k, v, w)
def reduce_order(fs, hi):
    return bit_orders(fs)[hi][::-1]


def reduce_masks(fs, hi):
    return combos(reduce_order(fs, hi)[1:][::-1])


def first_copies(hi, fs, f, view, land, ssem, rsem):
    bit = reduce_order(fs, hi)[0]
    return [remote(view(flip(flip(f, m), bit)), land(i), ssem.at[i], rsem.at[i], fsdp=flip(f, bit))
            for i, m in enumerate(reduce_masks(fs, hi))]


def later_copies(hi, stage, fs, f, held, land, ssem, rsem):
    bit = reduce_order(fs, hi)[stage]
    keep = fs >> (stage + 1)
    base = fs // 2 - (fs >> stage)
    return [remote(held(keep + i), land(base + i), ssem.at[base + i], rsem.at[base + i], fsdp=flip(f, bit)) for i in range(keep)]


def add_low(a, b):
    return (a.astype(F32) + b.astype(F32)).astype(BF16)


def early_parts(nz):
    return (nz - 1, 0) if nz > 1 else (0,)


def late_parts(nz):
    return tuple(t for t in range(nz - 2, 0, -1))


def rope_norm_back(g, pre, gain, cos, sins):
    c = g * cos + pltpu.roll(g * sins, HEAD // 2, 1)
    inv = lax.rsqrt(jnp.mean(pre * pre, axis=-1, keepdims=True) + EPS)
    n = pre * inv
    sc = c * gain
    return inv * (sc - n * jnp.mean(sc * n, axis=-1, keepdims=True)), c * n


def attend_back_kernel(dims, slot_ref, block_ref, q_ref, k_ref, v_ref, o_ref, l_ref, do_ref, pre_ref, cos_ref, sin_ref,
                       qg_ref, kg_ref, re_ref, g_ref, d_ref, te_ref, tl_ref, qgg_ref, kgg_ref,
                       dq, dk, dv, dl, held, rl, rn, ls, fss, fsr, nss, nsr):
    fs, nc, nz = dims
    f = lax.axis_index("fsdp")
    heads = q_ref.shape[2] // HEAD
    early, late = early_parts(nz), late_parts(nz)
    stages = fs.bit_length() - 1
    barrier = pltpu.get_barrier_semaphore()
    bits = bit_orders(fs)[0]
    for bit in bits:
        pl.semaphore_signal(barrier, inc=1, device_id={"fsdp": flip(f, bit)}, device_id_type=MESH)
    own = []
    for e, t in enumerate(early + late):
        for hi in range(2):
            for i, m in enumerate(reduce_masks(fs, hi)):
                own.append(pltpu.make_async_copy(g_ref.at[t, flip(f, m), hi], held.at[e, hi, i], ls.at[e, hi, i]))
    for cp in own:
        cp.start()
    pl.semaphore_wait(barrier, len(bits))

    def first(j, hi):
        return first_copies(hi, fs, f, lambda g: g_ref.at[late[j], g, hi], lambda i: rl.at[j, hi, i], fss.at[j, hi], fsr.at[j, hi])

    def later(e, hi, stage):
        return later_copies(hi, stage, fs, f, lambda i: held.at[e, hi, i], lambda i: rn.at[e, hi, i], nss.at[e, hi], nsr.at[e, hi])
    for cp in own:
        cp.wait()
    for e in range(len(early)):
        for hi in range(2):
            held[e, hi] = add_low(held[e, hi], re_ref[e, hi])
            if stages > 1:
                for cp in later(e, hi, 1):
                    cp.start()
    for j in range(len(late)):
        for hi in range(2):
            for cp in first(j, hi):
                cp.start()

    key_at = lax.broadcasted_iota(jnp.int32, (BLOCK, BLOCK), 0)
    tri = key_at <= lax.broadcasted_iota(jnp.int32, (BLOCK, BLOCK), 1)
    dk[...] = jnp.zeros_like(dk)
    dv[...] = jnp.zeros_like(dv)
    for qb in range(BLOCKS):
        at = slot_ref[qb]
        q2, g2 = stack_heads(q_ref[at]), stack_heads(do_ref[at])
        dl[...] = jnp.broadcast_to(jnp.sum((g2.astype(F32) * stack_heads(o_ref[at]).astype(F32)).T, axis=0, keepdims=True), dl.shape)

        def pair(kb, diagonal):
            k = k_ref[slot_ref[kb]]
            v = v_ref[slot_ref[kb], :, :HEAD]
            p = jnp.exp2(dot(k, q2, NT) - l_ref[qb, 0:1])
            if diagonal:
                p = jnp.concatenate([jnp.where(tri, p[:, h * BLOCK:(h + 1) * BLOCK], 0.0) for h in range(heads)], axis=1)
            ds = (p * (dot(v, g2, NT) - dl[0:1])).astype(BF16)
            dv[kb] += dot(p.astype(BF16), g2, NN)
            dk[kb] += dot(ds, q2, NN)
            return dot(ds, k, TN)
        total = pair(qb, True)
        if full_keys(qb):
            total = lax.fori_loop(0, full_keys(qb), lambda kb, t: t + pair(kb, False), total)
        dq[qb] = total

    qgg_ref[...] = jnp.zeros_like(qgg_ref)
    kgg_ref[...] = jnp.zeros_like(kgg_ref)

    @pl.loop(0, BLOCKS)
    def _(s):
        b = block_ref[s]
        at = s
        cos, sins = cos_ref[at], sin_ref[at]
        qs = dq[b]
        for h in range(heads):
            back, part = rope_norm_back(qs[h * BLOCK:(h + 1) * BLOCK] * HEAD ** -0.5, pre_ref[at, :, h * HEAD:(h + 1) * HEAD].astype(F32), qg_ref[...], cos, sins)
            d_ref[at, :, h * HEAD:(h + 1) * HEAD] = back.astype(BF16)
            qgg_ref[...] += jnp.sum(part, axis=0, keepdims=True)
        back, part = rope_norm_back(dk[b] * (1.0 / LOG2E), pre_ref[at, :, heads * HEAD:].astype(F32), kg_ref[...], cos, sins)
        d_ref[at, :, heads * HEAD:(heads + 1) * HEAD] = back.astype(BF16)
        kgg_ref[...] += jnp.sum(part, axis=0, keepdims=True)
        d_ref[at, :, (heads + 1) * HEAD:] = dv[b].astype(BF16)

    for stage in range(1, stages):
        keep = fs >> (stage + 1)
        base = fs // 2 - (fs >> stage)
        for e in range(len(early)):
            for hi in range(2):
                for cp in later(e, hi, stage):
                    cp.wait_recv()
                held[e, hi, :keep] = add_low(held[e, hi, :keep], rn[e, hi, base:base + keep])
                if stage + 1 < stages:
                    for cp in later(e, hi, stage + 1):
                        cp.start()
    for e in range(len(early)):
        te_ref[e] = held[e, :, 0]
    for j in range(len(late)):
        for hi in range(2):
            for cp in first(j, hi):
                cp.wait_recv()
            tl_ref[j, hi] = add_low(held[len(early) + j, hi], rl[j, hi])
    for j in range(len(late)):
        for hi in range(2):
            for cp in first(j, hi):
                cp.wait_send()
    for e in range(len(early)):
        for hi in range(2):
            for stage in range(1, stages):
                for cp in later(e, hi, stage):
                    cp.wait_send()


def attend_back_call(dims, slot, block, q, k, v, o, l, do, pre, cos, sin, qg, kg, re, g):
    fs, nc, nz = dims
    q_cols = q.shape[2]
    heads = q_cols // HEAD
    early, late = len(early_parts(nz)), len(late_parts(nz))
    shard, cols = g.shape[3:]
    DMA = pltpu.SemaphoreType.DMA
    V = pltpu.VMEM
    return pl.pallas_call(
        lambda *refs: attend_back_kernel(dims, *refs),
        out_shape=(
            jax.ShapeDtypeStruct((BLOCKS, BLOCK, q_cols + 2 * HEAD), BF16),
            jax.ShapeDtypeStruct((early, 2, shard, cols), BF16),
            jax.ShapeDtypeStruct((late, 2, fs // 2, shard, cols), BF16),
            jax.ShapeDtypeStruct((1, HEAD), F32),
            jax.ShapeDtypeStruct((1, HEAD), F32),
        ),
        in_specs=[SMEM_SPEC, SMEM_SPEC] + [VMEM_SPEC] * 12 + [ANY_SPEC],
        out_specs=(VMEM_SPEC,) * 5,
        scratch_shapes=[
            V((BLOCKS, heads * BLOCK, HEAD), F32), V((BLOCKS, BLOCK, HEAD), F32), V((BLOCKS, BLOCK, HEAD), F32),
            V((8, heads * BLOCK), F32),
            V((nz, 2, fs // 2, shard, cols), BF16), V((late, 2, fs // 2, shard, cols), BF16),
            V((early, 2, max(fs // 2 - 1, 1), shard, cols), BF16),
            DMA((nz, 2, fs // 2)), DMA((late, 2, fs // 2)), DMA((late, 2, fs // 2)),
            DMA((early, 2, max(fs // 2 - 1, 1))), DMA((early, 2, max(fs // 2 - 1, 1))),
        ],
        compiler_params=pltpu.CompilerParams(collective_id=3, has_side_effects=True, vmem_limit_bytes=VMEM_LIMIT),
        cost_estimate=pl.CostEstimate(flops=2 * 20 * BLOCK * BLOCK * heads * 5 * HEAD, bytes_accessed=40 * 2**20, transcendentals=0),
    )(slot, block, q, k, v, o, l, do, pre, cos, sin, qg, kg, re, g)
def column_parts(dims, hidden, q_cols):
    return (0, hidden, 2 * hidden, 3 * hidden, 3 * hidden + q_cols)


def feed_kernel(dims, x_ref, dy_ref, o_ref, w_ref, gain_ref, out_ref, dh_ref, fg_ref, do_ref, g_ref, re_ref,
                wb, hs, b_ref, da_ref, dgu, u_ref, acc, dacc, snd, rcv, dos, bt, yt, at,
                ls, gs, ss, sr, xs, xr, fss, fsr):
    fs, nc, nz = dims
    f, c, z = lax.axis_index("fsdp"), lax.axis_index("ctx"), lax.axis_index("tp")
    o = 1 - c
    rows, width = x_ref.shape
    q_cols = o_ref.shape[3]
    hidden = (w_ref.shape[2] - q_cols) // 3
    gate, up_, down_, out_, end = column_parts(dims, hidden, q_cols)
    loads = [pltpu.make_async_copy(w_ref.at[zz], wb.at[zz], ls.at[zz]) for zz in range(nz)]
    for cp in loads:
        cp.start()
    barrier = pltpu.get_barrier_semaphore()
    pl.semaphore_signal(barrier, inc=1, device_id={"ctx": o}, device_id_type=MESH)
    for dz in range(1, nz):
        pl.semaphore_signal(barrier, inc=1, device_id={"tp": lax.rem(z + dz, nz)}, device_id_type=MESH)
    bit_first = sorted({reduce_order(fs, hi)[0] for hi in range(2)}) if fs > 1 else []
    for bit in bit_first:
        pl.semaphore_signal(barrier, inc=1, device_id={"fsdp": flip(f, bit)}, device_id_type=MESH)
    pl.semaphore_wait(barrier, nz + len(bit_first))
    early = early_parts(nz)
    shard = width // (fs * nc)

    def first(e, hi):
        def view(g):
            return wb.at[early[e], pl.ds(pl.multiple_of((g * nc + hi) * shard, shard), shard)]
        return first_copies(hi, fs, f, view, lambda i: re_ref.at[e, hi, i], fss.at[e, hi], fsr.at[e, hi])

    def cross(i, src, dst):
        return remote(src, dst, ss.at[i], sr.at[i], ctx=o)
    for cp in loads:
        cp.wait()

    def project(side):
        total = dot(o_ref[0, side], wb[0, :, out_:end], NT)
        for zz in range(1, nz):
            total += dot(o_ref[zz, side], wb[zz, :, out_:end], NT)
        return total
    snd[0] = project(o).astype(BF16)
    cross(0, snd.at[0], rcv.at[0]).start()
    own = project(c)
    cross(0, snd.at[0], rcv.at[0]).wait_recv()
    h = x_ref[...].astype(F32) + own + rcv[0].astype(F32)
    hs[...] = h
    b_ref[c] = (h * lax.rsqrt(jnp.mean(h * h, axis=-1, keepdims=True) + EPS) * gain_ref[...]).astype(BF16)
    cross(1, b_ref.at[c], b_ref.at[c]).start()
    yt[...] = dy_ref[...].reshape(nc * rows, width).T
    cross(1, b_ref.at[c], b_ref.at[o]).wait_recv()

    @pl.loop(0, nz)
    def _(zz):
        both = b_ref[...].reshape(nc * rows, width)
        gu = dot(both, wb[zz, :, gate:down_], NN)
        du = dot(dy_ref[...].reshape(nc * rows, width), wb[zz, :, down_:out_], NN)
        gt, uv = gu[:, :hidden], gu[:, hidden:]
        sig = 1.0 / (1.0 + jnp.exp(-gt))
        silu = gt * sig
        hid = (silu * uv).astype(BF16)
        u_ref[zz] = hid
        dgu[zz, :, :hidden] = (du * uv * sig * (1.0 + gt * (1.0 - sig))).astype(BF16)
        dgu[zz, :, hidden:] = (du * silu).astype(BF16)

        @pl.when(zz == 0)
        def _():
            acc[...] = dot(hid, wb[zz, :, down_:out_], NT)
            dacc[...] = dot(dgu[zz], wb[zz, :, gate:down_], NT)

        @pl.when(zz > 0)
        def _():
            acc[...] += dot(hid, wb[zz, :, down_:out_], NT)
            dacc[...] += dot(dgu[zz], wb[zz, :, gate:down_], NT)

    def side_rows(side):
        return pl.ds(pl.multiple_of(side * rows, 128), rows)
    snd[1] = dacc[side_rows(o)].astype(BF16)
    cross(2, snd.at[1], rcv.at[1]).start()
    snd[2] = acc[side_rows(o)].astype(BF16)
    cross(3, snd.at[2], rcv.at[2]).start()
    bt[...] = b_ref[...].reshape(nc * rows, width).T
    cross(2, snd.at[1], rcv.at[1]).wait_recv()
    db = dacc[side_rows(c)] + rcv[1].astype(F32)
    h = hs[...]
    inv = lax.rsqrt(jnp.mean(h * h, axis=-1, keepdims=True) + EPS)
    n = h * inv
    sc = db * gain_ref[...]
    dh = dy_ref[c].astype(F32) + inv * (sc - n * jnp.mean(sc * n, axis=-1, keepdims=True))
    fg_ref[...] = jnp.sum(db * n, axis=0, keepdims=True)
    dh_ref[...] = dh
    da_ref[c] = dh.astype(BF16)
    cross(4, da_ref.at[c], da_ref.at[c]).start()
    cross(3, snd.at[2], rcv.at[2]).wait_recv()
    out_ref[...] = (hs[...] + acc[side_rows(c)] + rcv[2].astype(F32)).astype(BF16)
    cross(4, da_ref.at[c], da_ref.at[o]).wait_recv()

    @pl.loop(1, nz + 1)
    def _(dz):
        to = lax.rem(z + dz, nz)
        dos[to] = dot(da_ref[...].reshape(nc * rows, width), wb[to, :, out_:end], NN).astype(BF16).reshape(nc, rows, q_cols)

        @pl.when(dz < nz)
        def _():
            for side in range(nc):
                remote(dos.at[to, side], do_ref.at[side, z], xs.at[dz, side], xr.at[z, side], tp=to).start()
    for side in range(nc):
        do_ref[side, z] = dos[z, side]
    at[...] = da_ref[...].reshape(nc * rows, width).T

    for zz in early + late_parts(nz):
        wb[zz, :, gate:down_] = dot(bt[...], dgu[zz], NN).astype(BF16)
        wb[zz, :, down_:out_] = dot(yt[...], u_ref[zz], NN).astype(BF16)
        wb[zz, :, out_:end] = dot(at[...], o_ref[zz].reshape(nc * rows, q_cols), NN).astype(BF16)
        pltpu.make_async_copy(wb.at[zz], g_ref.at[zz], gs.at[zz]).start()
        if zz in early:
            for hi in range(2):
                for cp in first(early.index(zz), hi):
                    cp.start()
    for zz in range(nz):
        pltpu.make_async_copy(wb.at[zz], g_ref.at[zz], gs.at[zz]).wait()
    for dz in range(1, nz):
        src = lax.rem(z + dz, nz)
        for side in range(nc):
            cp = remote(dos.at[0, side], do_ref.at[side, src], xs.at[dz, side], xr.at[src, side], tp=src)
            cp.wait_recv()
            cp.wait_send()
    for e in range(len(early)):
        for hi in range(2):
            for cp in first(e, hi):
                cp.wait_recv()
                cp.wait_send()
    for i, part in enumerate((snd.at[0], b_ref.at[c], snd.at[1], snd.at[2], da_ref.at[c])):
        cross(i, part, part).wait_send()


def feed_call(dims, x, dyp, o, w, gain):
    fs, nc, nz = dims
    rows, width = x.shape
    q_cols = o.shape[3]
    cols = w.shape[2]
    hidden = (cols - q_cols) // 3
    early = len(early_parts(nz))
    DMA = pltpu.SemaphoreType.DMA
    V = pltpu.VMEM
    return pl.pallas_call(
        lambda *refs: feed_kernel(dims, *refs),
        out_shape=(
            jax.ShapeDtypeStruct((rows, width), BF16),
            jax.ShapeDtypeStruct((rows, width), F32),
            jax.ShapeDtypeStruct((1, width), F32),
            jax.ShapeDtypeStruct((nc, nz, rows, q_cols), BF16),
            jax.ShapeDtypeStruct(w.shape, BF16),
            jax.ShapeDtypeStruct((early, 2, fs // 2, width // (fs * nc), cols), BF16),
        ),
        in_specs=[VMEM_SPEC] * 3 + [ANY_SPEC, VMEM_SPEC],
        out_specs=(VMEM_SPEC,) * 4 + (ANY_SPEC, ANY_SPEC),
        scratch_shapes=[
            V(w.shape, BF16), V((rows, width), F32), V((nc, rows, width), BF16), V((nc, rows, width), BF16),
            V((nz, nc * rows, 2 * hidden), BF16), V((nz, nc * rows, hidden), BF16),
            V((nc * rows, width), F32), V((nc * rows, width), F32),
            V((3, rows, width), BF16), V((3, rows, width), BF16), V((nz, nc, rows, q_cols), BF16),
            V((width, nc * rows), BF16), V((width, nc * rows), BF16), V((width, nc * rows), BF16),
            DMA((nz,)), DMA((nz,)), DMA((5,)), DMA((5,)), DMA((nz, nc)), DMA((nz, nc)),
            DMA((early, 2, fs // 2)), DMA((early, 2, fs // 2)),
        ],
        compiler_params=pltpu.CompilerParams(collective_id=2, has_side_effects=True, vmem_limit_bytes=VMEM_LIMIT),
        cost_estimate=pl.CostEstimate(flops=2 * 13 * 2**30, bytes_accessed=40 * 2**20, transcendentals=0),
    )(x, dyp, o, w, gain)
def line_events(nz):
    out = []
    for z in range(nz):
        events = [(z + nz - 1 - t, 0, t) for t in range(z + 1, nz)] + [(nz - 1 - z + t, 1, t) for t in range(z)]
        out.append([(way, t) for _, way, t in sorted(events)])
    return out


def at_place(z, rows):
    return pick(z, rows)


def finish_kernel(dims, d_ref, wall_ref, a_ref, x_ref, dh_ref, gain_ref, te_ref, tl_ref, fg_ref, qgg_ref, kgg_ref,
                  ig_ref, dwq_ref, dwz_ref, gains_ref,
                  pa, sib, ru, sa, snd, rq, wq, rw, sw, tw, rn, fin, share, sc_, gx, gy,
                  bs, br, us, ur, qs, qr, vs, vr, ns, nr, cs, cr, hs, hr):
    fs, nc, nz = dims
    f, c, z = lax.axis_index("fsdp"), lax.axis_index("ctx"), lax.axis_index("tp")
    o = 1 - c
    me = f * nc + c
    rows, width = x_ref.shape
    shard = dwq_ref.shape[1]
    early, late = early_parts(nz), late_parts(nz)
    stages = fs.bit_length() - 1
    others = [(df, dc) for df in range(fs) for dc in range(nc) if (df, dc) != (0, 0)]
    barrier = pltpu.get_barrier_semaphore()
    for df, dc in others:
        pl.semaphore_signal(barrier, inc=1, device_id={"fsdp": lax.rem(f + df, fs), "ctx": lax.rem(c + dc, nc)}, device_id_type=MESH)
    for dz in range(1, nz):
        pl.semaphore_signal(barrier, inc=1, device_id={"tp": lax.rem(z + dz, nz)}, device_id_type=MESH)
    pl.semaphore_wait(barrier, len(others) + nz - 1)

    def later(j, hi, stage):
        return later_copies(hi, stage, fs, f, lambda i: tl_ref.at[j, hi, i], lambda i: rn.at[j, hi, i], ns.at[j, hi], nr.at[j, hi])
    for j in range(len(late)):
        for hi in range(2):
            if stages > 1:
                for cp in later(j, hi, 1):
                    cp.start()

    order = sorted(range(nz), key=lambda t: (min(t, nz - 1 - t), -t))

    def cross(t):
        return remote(snd.at[t], sib.at[t], bs.at[t], br.at[t], ctx=o)

    @pl.loop(0, nz)
    def _(i):
        t = pick(i, order)
        snd[t] = dot(d_ref[o * nz + t], wall_ref[...], NT).astype(BF16)
        cross(t).start()
        pa[t] = dot(d_ref[c * nz + t], wall_ref[...], NT)

    @pl.loop(0, nz)
    def _(i):
        t = pick(i, order)
        cross(t).wait_recv()
        pa[t] += sib[t].astype(F32)

    events = line_events(nz)

    def event(i):
        way = at_place(z, [events[zz][i][0] for zz in range(nz)])
        t = at_place(z, [events[zz][i][1] for zz in range(nz)])
        arrives = jnp.where(way == 0, z > 0, z < nz - 1)
        to = jnp.where(way == 0, jnp.minimum(z + 1, nz - 1), jnp.maximum(z - 1, 0))
        slot = jnp.where((way == 1) & (t == to), nz, t)
        return t, arrives, to, slot

    def rows_copy(i):
        _, _, to, slot = event(i)
        return remote(sa.at[i], ru.at[slot], us.at[i], ur.at[slot], tp=to)

    def rows_event(i):
        t, arrives, _, _ = event(i)

        @pl.when(arrives)
        def _():
            remote(sa.at[i], ru.at[t], us.at[i], ur.at[t], ctx=o).wait_recv()
            sa[i] = (pa[t] + ru[t].astype(F32)).astype(BF16)

        @pl.when(jnp.logical_not(arrives))
        def _():
            sa[i] = pa[t].astype(BF16)
        rows_copy(i).start()

    def weights(r):
        return pl.ds(pl.multiple_of(r * shard, shard), shard)

    rows_event(0)
    wq[...] = jnp.zeros_like(wq)

    @pl.loop(0, nc * nz)
    def _(s):
        wq[...] += dot(a_ref[s], d_ref[s], TN)
    rq[me] = wq[weights(me)].astype(BF16)
    for i, (df, dc) in enumerate(others):
        tf, tc = lax.rem(f + df, fs), lax.rem(c + dc, nc)
        sc_[i] = wq[weights(tf * nc + tc)].astype(BF16)
        remote(sc_.at[i], rq.at[me], qs.at[i], qr.at[me], fsdp=tf, ctx=tc).start()
    for e in range(len(early)):
        tw[early[e]] = te_ref[e]
    for stage in range(1, stages):
        keep = fs >> (stage + 1)
        base = fs // 2 - (fs >> stage)
        for j in range(len(late)):
            for hi in range(2):
                for cp in later(j, hi, stage):
                    cp.wait_recv()
                if stage + 1 == stages:
                    tw[late[j], hi] = add_low(tl_ref[j, hi, 0], rn[j, hi, base])
                else:
                    tl_ref[j, hi, :keep] = add_low(tl_ref[j, hi, :keep], rn[j, hi, base:base + keep])
                    for cp in later(j, hi, stage + 1):
                        cp.start()
    for i in range(1, nz - 1):
        rows_event(i)

    def grads_copy(i):
        _, _, to, slot = event(i)
        return remote(sw.at[i], rw.at[slot], vs.at[i], vr.at[slot], tp=to)

    def grads_event(i):
        t, arrives, _, _ = event(i)

        @pl.when(arrives)
        def _():
            remote(sw.at[i], rw.at[t], vs.at[i], vr.at[t], ctx=o).wait_recv()
            sw[i] = add_low(tw[t], rw[t])

        @pl.when(jnp.logical_not(arrives))
        def _():
            sw[i] = tw[t]
        grads_copy(i).start()
    grads_event(0)

    def rows_arrival(way):
        slot = nz if way else z
        return remote(sa.at[0], ru.at[slot], us.at[0], ur.at[slot], ctx=o)

    @pl.when(z > 0)
    def _():
        rows_arrival(0).wait_recv()
        pa[z] += ru[z].astype(F32)

    @pl.when(z < nz - 1)
    def _():
        rows_arrival(1).wait_recv()
        pa[z] += ru[nz].astype(F32)
    da = pa[z]
    x = x_ref[...].astype(F32)
    inv = lax.rsqrt(jnp.mean(x * x, axis=-1, keepdims=True) + EPS)
    n = x * inv
    sc = da * gain_ref[...]
    ig_ref[...] = dh_ref[...] + inv * (sc - n * jnp.mean(sc * n, axis=-1, keepdims=True))
    gx[z, 0:1] = jnp.sum(da * n, axis=0, keepdims=True)
    gx[z, 1:2] = fg_ref[...]
    gx[z, 2:3] = jnp.concatenate([qgg_ref[...], kgg_ref[...]] + [jnp.zeros((1, width - 2 * HEAD), F32)], axis=1)
    gx[z, 3:] = jnp.zeros_like(gx[z, 3:])
    for dz in range(1, nz):
        to = lax.rem(z + dz, nz)
        remote(gx.at[z], gx.at[z], hs.at[dz - 1], hr.at[z], tp=to).start()
    for i in range(1, nz - 1):
        grads_event(i)

    for i, (df, dc) in enumerate(others):
        src = lax.rem(f + df, fs) * nc + lax.rem(c + dc, nc)
        remote(sc_.at[0], rq.at[src], qs.at[i], qr.at[src], ctx=o).wait_recv()
    for cc in range(nc):
        total = rq[cc].astype(F32)
        for ff in range(1, fs):
            total += rq[ff * nc + cc].astype(F32)
        dwq_ref[cc] = total

    def grads_arrival(way):
        slot = nz if way else z
        return remote(sw.at[0], rw.at[slot], vs.at[0], vr.at[slot], ctx=o)

    for dz in range(1, nz):
        src = lax.rem(z + dz, nz)
        remote(gx.at[src], gx.at[src], hs.at[dz - 1], hr.at[src], tp=src).wait_recv()
    total = gx[0]
    for zz in range(1, nz):
        total += gx[zz]
    gy[me] = total
    for i, (df, dc) in enumerate(others):
        remote(gy.at[me], gy.at[me], hs.at[nz - 1 + i], hr.at[nz + me], fsdp=lax.rem(f + df, fs), ctx=lax.rem(c + dc, nc)).start()

    fin[...] = tw[z].astype(F32)

    @pl.when(z > 0)
    def _():
        grads_arrival(0).wait_recv()
        fin[...] += rw[z].astype(F32)

    @pl.when(z < nz - 1)
    def _():
        grads_arrival(1).wait_recv()
        fin[...] += rw[nz].astype(F32)
    share[0] = fin[o].astype(BF16)
    swap = remote(share.at[0], share.at[1], cs.at[0], cr.at[0], ctx=o)
    swap.start()
    dwz_ref[c] = fin[c]

    for i, (df, dc) in enumerate(others):
        src = lax.rem(f + df, fs) * nc + lax.rem(c + dc, nc)
        remote(gy.at[src], gy.at[src], hs.at[nz - 1 + i], hr.at[nz + src], ctx=o).wait_recv()
    total = gy[0]
    for r in range(1, fs * nc):
        total += gy[r]
    gains_ref[...] = total
    swap.wait_recv()
    dwz_ref[o] = share[1].astype(F32)

    swap.wait_send()
    for i in range(nz - 1):
        rows_copy(i).wait_send()
        grads_copy(i).wait_send()
    for t in range(nz):
        cross(t).wait_send()
    for i in range(nz - 1):
        remote(gx.at[0], gx.at[0], hs.at[i], hr.at[0], ctx=o).wait_send()
    for i in range(len(others)):
        remote(sc_.at[0], rq.at[0], qs.at[i], qr.at[0], ctx=o).wait_send()
        remote(gy.at[0], gy.at[0], hs.at[nz - 1 + i], hr.at[nz], ctx=o).wait_send()
    for j in range(len(late)):
        for hi in range(2):
            for stage in range(1, stages):
                for cp in later(j, hi, stage):
                    cp.wait_send()


def finish_call(dims, d, wall, a, x, dh, gain, te, tl, fg, qgg, kgg):
    fs, nc, nz = dims
    rows, width = x.shape
    shard, cols = te.shape[2:]
    proj = wall.shape[1]
    late = len(late_parts(nz))
    n = fs * nc
    DMA = pltpu.SemaphoreType.DMA
    V = pltpu.VMEM
    return pl.pallas_call(
        lambda *refs: finish_kernel(dims, *refs),
        out_shape=(
            jax.ShapeDtypeStruct((rows, width), F32),
            jax.ShapeDtypeStruct((nc, width // n, proj), F32),
            jax.ShapeDtypeStruct((nc, shard, cols), F32),
            jax.ShapeDtypeStruct((8, width), F32),
        ),
        in_specs=[VMEM_SPEC] * 11,
        out_specs=(VMEM_SPEC,) * 4,
        scratch_shapes=[
            V((nz, rows, width), F32), V((nz, rows, width), BF16), V((nz + 1, rows, width), BF16),
            V((nz - 1, rows, width), BF16), V((nz, rows, width), BF16),
            V((n, width // n, proj), BF16), V((width, proj), F32),
            V((nz + 1, 2, shard, cols), BF16), V((nz - 1, 2, shard, cols), BF16), V((nz, 2, shard, cols), BF16),
            V((late, 2, max(fs // 2 - 1, 1), shard, cols), BF16),
            V((2, shard, cols), F32), V((2, shard, cols), BF16),
            V((n - 1, width // n, proj), BF16), V((nz, 8, width), F32), V((n, 8, width), F32),
            DMA((nz,)), DMA((nz,)), DMA((nz - 1,)), DMA((nz + 1,)),
            DMA((n - 1,)), DMA((n,)), DMA((nz - 1,)), DMA((nz + 1,)),
            DMA((late, 2, max(fs // 2 - 1, 1))), DMA((late, 2, max(fs // 2 - 1, 1))),
            DMA((1,)), DMA((1,)), DMA((nz - 1 + n - 1,)), DMA((nz + n,)),
        ],
        compiler_params=pltpu.CompilerParams(collective_id=4, has_side_effects=True, vmem_limit_bytes=VMEM_LIMIT),
        cost_estimate=pl.CostEstimate(flops=2 * 4 * 2**30, bytes_accessed=40 * 2**20, transcendentals=0),
    )(d, wall, a, x, dh, gain, te, tl, fg, qgg, kgg)
def on_device(dims, tokens, out_grad, block_slot, attn_gain, ffn_gain, query_gain, key_norm_gain,
              w_query, key_weight, value_weight, w_out, w_gate, w_up, w_down):
    fs, nc, nz = dims
    rows, width = tokens.shape
    shard = w_query.shape[0]
    block_ids = block_slot[0]
    slots = jnp.zeros((BLOCKS,), jnp.int32).at[block_ids].set(jnp.arange(BLOCKS, dtype=jnp.int32))
    start = jnp.minimum(block_ids, PBLOCKS) * BLOCK
    places = (start[:, None] + jnp.arange(BLOCK, dtype=jnp.int32)[None, :]).reshape(-1).astype(F32)
    freqs = ROPE_BASE ** (-(jnp.arange(0, HEAD, 2).astype(F32) / HEAD))
    angles = places[:, None] * freqs[None, :]
    cos, sin = jnp.cos(angles), jnp.sin(angles)
    cos = jnp.concatenate([cos, cos], axis=1)
    sins = jnp.concatenate([-sin, sin], axis=1)

    def halves(w):
        return jnp.stack(jnp.split(w, nc, axis=1))
    wqkv = jnp.concatenate([halves(w_query), halves(key_weight), halves(value_weight)], axis=2)
    wz = jnp.concatenate([halves(w_gate), halves(w_up), halves(w_down.T), halves(w_out.T)], axis=2)
    hidden, q_cols = w_gate.shape[1] // nc, w_query.shape[1] // nc
    ag, fg = attn_gain[None], ffn_gain[None]
    qg, kg = query_gain[None], key_norm_gain[None]

    a, q, k, v, pre, wall, w, dyp = gather_call(
        dims, tokens, out_grad, ag, wqkv, wz, cos.reshape(-1, rows, HEAD), sins.reshape(-1, rows, HEAD), qg, kg)
    blocks = lambda t: t.reshape(BLOCKS, BLOCK, -1)
    q, k, v, pre = blocks(q), blocks(k), blocks(v), blocks(pre)
    w, mixed, o, logs = attend_call(dims, slots, block_ids, q, k, v, w, rows)
    cols = w.shape[4]
    result, dh, ffn_part, do, g, re = feed_call(dims, tokens, dyp, mixed, w.reshape(nz, width, cols), fg)
    d, te, tl, q_part, k_part = attend_back_call(
        dims, slots, block_ids, q, k, v, blocks(o), logs, blocks(do), pre, blocks(cos), blocks(sins), qg, kg,
        re, g.reshape(nz, fs, nc, shard, cols))
    input_grad, dwq, dwz, gains = finish_call(
        dims, d.reshape(nc * nz, rows, -1), wall.reshape(width, -1), a, tokens, dh, ag, te, tl, ffn_part, q_part, k_part)

    def whole(g, at, n):
        return jnp.concatenate([g[i, :, at:at + n] for i in range(nc)], axis=1)
    return (
        result, input_grad, gains[0], gains[1], gains[2, :HEAD], gains[2, HEAD:2 * HEAD],
        whole(dwq, 0, q_cols), whole(dwq, q_cols, HEAD), whole(dwq, q_cols + HEAD, HEAD),
        whole(dwz, 3 * hidden, q_cols).T, whole(dwz, 0, hidden), whole(dwz, hidden, hidden), whole(dwz, 2 * hidden, hidden).T,
    )


def solution(mesh):
    dims = (mesh.shape["fsdp"], mesh.shape["ctx"], mesh.shape["tp"])
    everything, weights = ("fsdp", "ctx", "tp"), ("fsdp", "ctx")
    split, turned = P(weights, "tp"), P("tp", weights)
    return jax.shard_map(
        lambda *args: on_device(dims, *args),
        mesh=mesh,
        in_specs=(P(everything, None), P(everything, None), P("fsdp", None), P(), P(), P(), P(), split, split, split, turned, split, split, turned),
        out_specs=(P(everything, None), P(everything, None), P(), P(), P(), P(), split, split, split, turned, split, split, turned),
        check_vma=False,
    )
```

time: 1510 us -> 487 us (0.32)
  waiting for transfers between devices: 780 us -> 0 us
  Pallas kernels: 0 us -> 443 us
  matrix products: 260 us -> 0 us
  loops' own time: 177 us -> 0 us
  local copies, waits for them, and re-layouts: 111 us -> 13.5 us
  blocking collectives: 67.7 us -> 0 us
  other arithmetic: 80.5 us -> 22.1 us
    reduce_scatter x13 -> x0, waiting for transfers between devices: 464 us -> none  [the longest x1 60.6 us: on_device(): lax.psum_scatter(jnp.dot(mixed_low, out_full, preferred_element_type=jnp....]
    pallas_call x0 -> x5, Pallas kernels: none -> 443 us  [the longest x1 121 us: finish_call(): pl.pallas_call(lambda *refs: finish_kernel(dims, *refs), out_shape=(jax.S...]
    all_gather x11 -> x0, waiting for transfers between devices: 312 us -> none  [the longest x1 65.7 us: on_device(): ffn_all = lax.all_gather(ffn_low, 'tp', axis=0, tiled=True)]
    dot_general x98 -> x0, matrix products: 260 us -> none  [the longest x7 39.6 us: contract_rows(): lax.dot_general(left, right, (((0,), (0,)), ((), ())), preferred_element_...]
    another operation x65 -> x0, loops' own time: 177 us -> none  [the longest x3 58.8 us: forward_block(): lax.fori_loop(0, block_ids.shape[0], out_step, jnp.zeros((BLOCK_TOKENS, k...]
    dynamic_slice x124 -> x0, local copies, waits for them, and re-layouts: 52.7 us -> none  [the longest x18 10.6 us: key_step(): block_ids[index]]
    psum x1 -> x0, blocking collectives: 45 us -> none  [on_device(): lax.psum((jnp.sum(attn_gain_part, axis=0), jnp.sum(ffn_gain_part, axis=0)...]
    reduce_sum x19 -> x0, other arithmetic: 30.9 us -> none  [the longest x11 9.98 us: stats_visit(): return (peak, total * jnp.exp(peak_old - peak) + jnp.sum(weights, axis=-1))]
  transfers between devices with their start and end apart: 24 -> 0, of which waited for: 20 -> 0; matrix products, arithmetic and copies ran while one was open for 16% -> 0% of each run, Pallas kernels for 0% -> 0%
where the time goes in v1:
time: 487 us; the launch traced here: 480 us
  Pallas kernels  443 us (91%)
  other arithmetic  22.1 us (5%)
  local copies, waits for them, and re-layouts  13.5 us (3%)
    pallas_call x1, Pallas kernels, finish_call(): pl.pallas_call(lambda *refs: finish_kernel(dims, *refs), out_shape=(jax.S...  121 us
    pallas_call x1, Pallas kernels, attend_call(): pl.pallas_call(lambda *refs: attend_kernel(dims, *refs), out_shape=(jax.S...  114 us
    pallas_call x1, Pallas kernels, feed_call(): pl.pallas_call(lambda *refs: feed_kernel(dims, *refs), out_shape=(jax.Sha...  75.9 us
    pallas_call x1, Pallas kernels, gather_call(): pl.pallas_call(lambda *refs: gather_kernel(dims, *refs), out_shape=(jax.S...  72.8 us
    pallas_call x1, Pallas kernels, attend_back_call(): pl.pallas_call(lambda *refs: attend_back_kernel(dims, *refs), out_shape=(...  59.8 us
    neg x2, other arithmetic, on_device(): sins = jnp.concatenate([-sin, sin], axis=1)  11.5 us

profile of v1, /device:TPU:0, one launch (start us, length us, event | category | flops | bytes accessed | tf_op | source)
XLA Modules:
  0.0 480.1 jit_solution(17394455024416237810)
XLA Ops:
  0.7 1.1 copy.28
  1.8 1.0 slice_bitcast_fusion.11
  2.8 1.0 copy.29
  3.9 0.9 maximum_maximum_fusion.refs_4_
  5.7 5.7 %fusion = (f32[8,384,64]{2,1,0:T(8,128)S(1)}, f32[8,384,64]{2,1,0:T(8,128)S(1)}, f32[8,384,64]{2,1,0:T(8,128)S(1)}) fusion(f32[64]{0:T(128)S(1)} %negate_power_fusion, f32[8,384]{1,0:T(8,128)S(1)} %convert_element_type.21), kind=kLoop, calls=%fused_computation.10 | loop fusion | flops 393216 | bytes 2371840 | tf_op jit(solution)/shard_map/neg | solution.py:1031
  11.4 2.5 pad_maximum_fusion
  13.9 72.8 %shard_map.237 = (bf16[8,384,1024]{2,1,0:T(8,128)(2,1)}, bf16[8,384,256]{2,1,0:T(8,128)(2,1)}, bf16[8,384,128]{2,1,0:T(8,128)(2,1)}, bf16[8,384,256]{2,1,0:T(8,1...) custom-call(bf16[384,1024]{1,0:T(8,128)(2,1)} %refs_3_.1, ...), custom_call_target="tpu_custom_call" | custom-call | flops 3221225472 | bytes 31457280 | tf_op jit(solution)/shard_map/pallas_call | solution.py:228
  86.8 1.4 scatter_custom_fusion.refs_0_
  88.2 113.6 %shard_map.238 = (bf16[4,4,2,128,1408]{4,3,2,1,0:T(8,128)(2,1)}, bf16[4,2,384,256]{3,2,1,0:T(8,128)(2,1)}, bf16[3072,256]{1,0:T(8,128)(2,1)}, f32[6,8,1024]{2,1,0:T(8,128)}) custom-call(s32[6]{0:T(128)} %scatter_custom_fusion.refs_0_, s32[6]{0:T(128)} %bitcast.95, bf16[6,512,256]{2,1,0:T(8,128)(2,1)} %bitcast.105, ...), custom_call_target="tpu_custom_call", output_to_operand_aliasing={{0}: (5, {})} | custom-call | flops 8053063680 | bytes 31457280 | tf_op jit(solution)/shard_map/pallas_call | solution.py:382
  201.8 75.9 %shard_map.239 = (bf16[384,1024]{1,0:T(8,128)(2,1)}, f32[384,1024]{1,0:T(8,128)}, f32[1,1024]{1,0:T(1,128)}, bf16[2,4,384,256]{3,2,1,0:T(8,128)(2,1)}, bf16[4,10...) custom-call(bf16[384,1024]{1,0:T(8,128)(2,1)} %refs_3_.1, bf16[2,384,1024]{2,1,0:T(8,128)(2,1)} %get-tuple-element.40.refs_1_, ...), custom_call_target="tpu_custom_call" | custom-call | flops 27917287424 | bytes 41943040 | tf_op jit(solution)/shard_map/pallas_call | solution.py:728
  277.7 5.9 %fusion.1 = (f32[6,512,64]{2,1,0:T(8,128)S(1)}, f32[6,512,64]{2,1,0:T(8,128)S(1)}, f32[6,512,64]{2,1,0:T(8,128)S(1)}) fusion(f32[64]{0:T(128)S(1)} %negate_power_fusion, f32[6,512]{1,0:T(8,128)S(1)} %add_convert_fusion), kind=kLoop, calls=%fused_computation.11 | loop fusion | flops 393216 | bytes 2371840 | tf_op jit(solution)/shard_map/neg | solution.py:1031
  283.6 2.6 pad_maximum_fusion.2
  286.2 59.8 %shard_map.240 = (bf16[6,512,512]{2,1,0:T(8,128)(2,1)}, bf16[2,2,128,1408]{3,2,1,0:T(8,128)(2,1)}, bf16[2,2,2,128,1408]{4,3,2,1,0:T(8,128)(2,1)}, f32[1,128]{1,0:T(1,128)}, f32[1,128]{1,0:T(1,128)}) custom-call(s32[6]{0:T(128)} %scatter_custom_fusion.refs_0_, s32[6]{0:T(128)} %bitcast.96, bf16[6,512,256]{2,1,0:T(8,128)(2,1)} %bitcast.106, ...), custom_call_target="tpu_custom_call" | custom-call | flops 13421772800 | bytes 41943040 | tf_op jit(solution)/shard_map/pallas_call | solution.py:559
  346.0 121.3 %shard_map.241 = (f32[384,1024]{1,0:T(8,128)}, f32[2,128,512]{2,1,0:T(8,128)}, f32[2,128,1408]{2,1,0:T(8,128)}, f32[8,1024]{1,0:T(8,128)}) custom-call(bf16[8,384,512]{2,1,0:T(8,128)(2,1)} %bitcast.103, bf16[1024,512]{1,0:T(8,128)(2,1)} %bitcast.111, bf16[8,384,1024]{2,1,0:T(8,128)(2,1)} %get-tuple-element.56.refs_2_, bf16[384,1024]{1,0:T(8,128)(2,1)} %refs_3_.1, ...), custom_call_target="tpu_custom_call" | custom-call | flops 8589934592 | bytes 41943040 | tf_op jit(solution)/shard_map/pallas_call | solution.py:992
  467.3 1.4 slice_bitcast_fusion.1
  468.8 0.9 copy.31
  469.7 0.8 pad_maximum_fusion.5
  470.5 0.8 pad_maximum_fusion.4
  471.2 1.0 slice_bitcast_fusion.7
  472.3 0.8 copy.30
  475.2 1.4 fusion.5
  476.6 1.2 slice_bitcast_fusion.28
  477.9 0.9 copy.35
  478.7 1.1 copy.36
  (34 shorter events, 3.1 us)
Async XLA Ops:
  0.6 3.2 copy-start.3
  1.8 3.1 copy-start.5
  1.8 3.1 copy-start.6
  1.8 3.1 copy-start.4
  3.9 1.8 copy-start.7
  469.7 3.4 copy-start.2
  472.2 5.6 %copy-start.1 = (bf16[384,1024]{1,0:T(8,128)(2,1)S(1)}, bf16[384,1024]{1,0:T(8,128)(2,1)}, u32[]{:S(2)}) copy-start(bf16[384,1024]{1,0:T(8,128)(2,1)} %get-tuple-element.139) | copy-start | bytes 2359300
  473.1 5.6 %copy-start = (f32[384,1024]{1,0:T(8,128)S(1)}, f32[384,1024]{1,0:T(8,128)}, u32[]{:S(2)}) copy-start(f32[384,1024]{1,0:T(8,128)} %get-tuple-element.140) | copy-start | bytes 4718596
